TPU v7x, 32 devices: a whole 2x2x4 slice. The times are simulated.
32 devices in a mesh: dp: 8 (over z, x), mp: 4 (over y, core).
Axes of the slice: x: 2, y: 2, z: 4, core: 2. Of those that a mesh axis runs over, the one named last changes fastest.
Arguments:
- token_ids: int32 [16, 512], P('dp'), may hold values from 0 to 42111
- seg_lengths: int32 [16, 4], P('dp'), may hold values from 1 to 256, 512 in all within a row
- counted: int32 [16, 512], P('dp'), may hold values from 0 to 1
- unit_slot: int32 [248], replicated, may hold values from 0 to 335, as said below
- master: float32 [336, 224, 1120], P('dp', 'mp'), may hold values from -1.07570575 to 1.07570575
- first_moment: float32 [336, 224, 1120], P('dp', 'mp'), may hold values from -8.443361e-05 to 8.443361e-05
- second_moment: float32 [336, 224, 1120], P('dp', 'mp'), may hold values from 8.4541124e-10 to 3.375216e-09
- norm_params: float32 [6, 1120], replicated, may hold values from -2 to 2
- norm_first: float32 [6, 1120], replicated, may hold values from -0.00068459683 to 0.00068459683
- norm_second: float32 [6, 1120], replicated, may hold values from 5.4646353e-08 to 2.1537093e-07
Outputs:
- new_master: float32 [336, 224, 1120], P('dp', 'mp')
- new_first: float32 [336, 224, 1120], P('dp', 'mp')
- new_second: float32 [336, 224, 1120], P('dp', 'mp')
- new_norms: float32 [6, 1120], replicated
- new_norm_first: float32 [6, 1120], replicated
- new_norm_second: float32 [6, 1120], replicated
- clip_norm: float32 [], replicated
- loss_sum: float32 [], replicated
- loss_count: float32 [], replicated
Inputs may be any that keep to these rules, and one draw needn't show every extreme that they name: Distinct values; block k is kept by index unit_slot[k] // 42 of dp; each index holds at most 42 blocks and one holds exactly 42.
All inputs are finite; a program needn't handle non-finite values.
Results may differ from a plain program's by a relative error of at most 0.0062.
The roundings to bfloat16 on the way count: a program that leaves them out, or rounds other values in their place, can miss the bound.
Values may be sent and summed in bfloat16 or wider, within the bound.
No kernel may reach another device: no remote copies, remote signals or barrier semaphores. Data moves between devices by JAX's collectives and lax.ppermute only.
A program may use at most 576 MiB of HBM per device.

v0:
```python
import jax
import jax.numpy as jnp
from jax import lax
from jax.sharding import PartitionSpec as P

HEADS = 20
HD = 56
FF = 4480
V = 42112
STEP = 10


NORM_EPS = 1e-05
LEARN_RATE = 0.1
BETA_ONE = 0.9
BETA_TWO = 0.95
ADAM_EPS = 1e-08
WEIGHT_DECAY = 0.1
CLIP_LIMIT = 1.0
NEG_FILL = -1e30


def joined(array, axis, combine):
    everything = jax.tree.map(lambda part: lax.all_gather(part, axis), array)
    initial = jax.tree.map(lambda part: part[0], everything)

    def hop(k, so_far):
        return combine(so_far, jax.tree.map(lambda part: part[k], everything))

    return lax.fori_loop(1, lax.axis_size(axis), hop, initial)


def layer_norm(x, gain, shift):
    centred = x - jnp.mean(x, axis=-1, keepdims=True)
    scale = lax.rsqrt(jnp.mean(centred * centred, axis=-1, keepdims=True) + NORM_EPS)
    return centred * scale * gain + shift


def segment_ids(lengths, span):
    bounds = jnp.cumsum(lengths)
    return jnp.sum(jnp.arange(span)[:, None] >= bounds[None, :], axis=1)


def contract_last(left, right):
    return lax.dot_general(
        left, right, (((1,), (1,)), ((), ())), preferred_element_type=jnp.float32
    )


def contract_first(left, right):
    return lax.dot_general(
        left, right, (((0,), (0,)), ((), ())), preferred_element_type=jnp.float32
    )


def branch_sum(value):
    return lax.psum(value, "mp")


def input_sum(value):
    return lax.psum(value, "mp")


def attention_probs(query, keys, seg):
    span = seg.shape[0]
    scores = jnp.einsum("qhd,khd->hqk", query, keys, preferred_element_type=jnp.float32) * HD ** (
        -0.5
    )
    place = jnp.arange(span)
    allowed = (seg[:, None] == seg[None, :]) & (place[None, :] <= place[:, None])
    scores = jnp.where(allowed[None], scores, NEG_FILL)
    expo = jnp.exp(scores - jnp.max(scores, axis=-1, keepdims=True))
    return expo / jnp.sum(expo, axis=-1, keepdims=True)


def forward_layer(x0, seg, gains, weights, heads):
    w_qkv, w_out, w_up, w_down = weights
    span = x0.shape[0]
    a1b = layer_norm(x0, gains[0], gains[1]).astype(jnp.bfloat16)
    qkv = contract_last(a1b, w_qkv).astype(jnp.bfloat16).reshape(span, 3, heads, HD)
    probs = attention_probs(qkv[:, 0], qkv[:, 1], seg)
    probs_low = probs.astype(jnp.bfloat16)
    mixed = jnp.einsum("hqk,khd->qhd", probs_low, qkv[:, 2], preferred_element_type=jnp.float32)
    mixed = mixed.reshape(span, heads * HD).astype(jnp.bfloat16)
    x1 = x0 + branch_sum(jnp.dot(mixed, w_out, preferred_element_type=jnp.float32))
    a2b = layer_norm(x1, gains[2], gains[3]).astype(jnp.bfloat16)
    pre = contract_last(a2b, w_up)
    hidden = jax.nn.gelu(pre).astype(jnp.bfloat16)
    x2 = x1 + branch_sum(jnp.dot(hidden, w_down, preferred_element_type=jnp.float32))
    return (x2, (a1b, qkv, probs, mixed, x1, a2b, pre, hidden))


def backward_layer(dx2, x0, gains, weights, heads, saved):
    w_qkv, w_out, w_up, w_down = weights
    a1b, qkv, kept, mixed, x1, a2b, pre, hidden = saved
    span = x0.shape[0]
    query, keys, values = (qkv[:, 0], qkv[:, 1], qkv[:, 2])
    dz = dx2.astype(jnp.bfloat16)
    d_down = contract_first(hidden, dz)
    d_hidden = contract_last(dz, w_down)
    d_pre = jax.vjp(jax.nn.gelu, pre)[1](d_hidden)[0].astype(jnp.bfloat16)
    d_up = contract_first(d_pre, a2b)
    d_a2 = input_sum(jnp.dot(d_pre, w_up, preferred_element_type=jnp.float32))
    dx1_norm, d_g2, d_b2 = jax.vjp(layer_norm, x1, gains[2], gains[3])[1](d_a2)
    dx1 = dx2 + dx1_norm
    dy = dx1.astype(jnp.bfloat16)
    d_out = contract_first(mixed, dy)
    d_mixed = contract_last(dy, w_out).astype(jnp.bfloat16).reshape(span, heads, HD)
    d_probs = jnp.einsum("qhd,khd->hqk", d_mixed, values, preferred_element_type=jnp.float32)
    d_values = jnp.einsum(
        "hqk,qhd->khd", kept.astype(jnp.bfloat16), d_mixed, preferred_element_type=jnp.float32
    )
    d_scores = (kept * (d_probs - jnp.sum(kept * d_probs, axis=-1, keepdims=True))).astype(
        jnp.bfloat16
    )
    d_query = jnp.einsum(
        "hqk,khd->qhd", d_scores, keys, preferred_element_type=jnp.float32
    ) * HD ** (-0.5)
    d_keys = jnp.einsum(
        "hqk,qhd->khd", d_scores, query, preferred_element_type=jnp.float32
    ) * HD ** (-0.5)
    d_qkv = (
        jnp.stack([d_query, d_keys, d_values], axis=1)
        .reshape(span, 3 * heads * HD)
        .astype(jnp.bfloat16)
    )
    d_qkv_weight = contract_first(d_qkv, a1b)
    d_a1 = input_sum(jnp.dot(d_qkv, w_qkv, preferred_element_type=jnp.float32))
    dx0_norm, d_g1, d_b1 = jax.vjp(layer_norm, x0, gains[0], gains[1])[1](d_a1)
    dx0 = dx1 + dx0_norm
    gain_grads = jnp.stack([d_g1, d_b1, d_g2, d_b2])
    return (dx0, (d_qkv_weight, d_out, d_up, d_down), gain_grads)


def slot_layout(grads, unit_slot, total_slots, rows_unit):
    blocks = grads.reshape(-1, rows_unit, grads.shape[1])
    return (
        jnp.zeros((total_slots, rows_unit, grads.shape[1]), jnp.float32).at[unit_slot].set(blocks)
    )


def adam_update(weight, grad, first, second, decay):
    first = BETA_ONE * first + (1.0 - BETA_ONE) * grad
    second = BETA_TWO * second + (1.0 - BETA_TWO) * grad * grad
    stride = first / (1.0 - BETA_ONE**STEP) / (jnp.sqrt(second / (1.0 - BETA_TWO**STEP)) + ADAM_EPS)
    return (weight - LEARN_RATE * (stride + decay * weight), first, second)


def merge_stats(left, right):
    top = jnp.maximum(left[0], right[0])
    total = left[1] * jnp.exp(left[0] - top) + right[1] * jnp.exp(right[0] - top)
    return (top, total, left[2] + right[2])


def per_device(
    token_ids,
    seg_lengths,
    counted,
    unit_slot,
    master,
    first_moment,
    second_moment,
    norm_params,
    norm_first,
    norm_second,
):
    slots, rows_unit, width = master.shape
    parts = lax.axis_size("mp")
    total_slots = slots * lax.axis_size("dp")
    heads = HEADS // parts
    q_rows = heads * HD
    ff_rows = FF // parts
    vocab_rows = V // parts
    vocab_start = lax.axis_index("mp") * vocab_rows
    root = width**0.5
    every = lax.all_gather(master.astype(jnp.bfloat16), "dp", axis=0, tiled=True)
    stacked = every[unit_slot].reshape(-1, width)
    weights = (
        stacked[: 3 * q_rows],
        stacked[3 * q_rows : 4 * q_rows],
        stacked[4 * q_rows : 4 * q_rows + ff_rows],
        stacked[4 * q_rows + ff_rows : 4 * q_rows + 2 * ff_rows],
    )
    table = stacked[4 * q_rows + 2 * ff_rows :]
    span = token_ids.shape[1]
    grads = jnp.zeros(stacked.shape, jnp.float32)
    gain_grads = jnp.zeros(norm_params.shape, jnp.float32)
    loss_sum = jnp.zeros((), jnp.float32)
    loss_count = jnp.zeros((), jnp.float32)
    vocab_iota = jnp.arange(vocab_rows)
    for micro in range(token_ids.shape[0]):
        ids = token_ids[micro]
        seg = segment_ids(seg_lengths[micro], span)
        local = ids - vocab_start
        inside = ((local >= 0) & (local < vocab_rows)).astype(jnp.float32)
        safe = jnp.clip(local, 0, vocab_rows - 1)
        x0 = branch_sum(table[safe].astype(jnp.float32) * (root * inside)[:, None])
        x2, saved = forward_layer(x0, seg, norm_params, weights, heads)
        final_low = layer_norm(x2, norm_params[4], norm_params[5]).astype(jnp.bfloat16)
        logits = contract_last(final_low, table)
        following = jnp.concatenate([ids[1:], ids[:1]]) - vocab_start
        keep = jnp.concatenate(
            [(seg[1:] == seg[:-1]) & (counted[micro][:-1] == 1), jnp.zeros((1,), bool)]
        ).astype(jnp.float32)
        onehot = vocab_iota[None, :] == following[:, None]
        picked = jnp.sum(jnp.where(onehot, logits, 0.0), axis=-1)
        top = jnp.max(logits, axis=-1)
        total = jnp.sum(jnp.exp(logits - top[:, None]), axis=-1)
        top, total, picked = joined((top, total, picked), "mp", merge_stats)
        lse = top + jnp.log(total)
        loss_sum = loss_sum + jnp.sum(keep * (lse - picked))
        loss_count = loss_count + jnp.sum(keep)
        d_logits = (
            keep[:, None] * (jnp.exp(logits - lse[:, None]) - onehot.astype(jnp.float32))
        ).astype(jnp.bfloat16)
        d_table = contract_first(d_logits, final_low)
        d_final = input_sum(jnp.dot(d_logits, table, preferred_element_type=jnp.float32))
        dx2, d_gf, d_bf = jax.vjp(layer_norm, x2, norm_params[4], norm_params[5])[1](d_final)
        dx0, layer_grads, layer_gains = backward_layer(dx2, x0, norm_params, weights, heads, saved)
        d_table = d_table.at[safe].add(dx0 * (root * inside)[:, None])
        micro_grads = jnp.concatenate(list(layer_grads) + [d_table], axis=0)
        gain_grads = gain_grads + jnp.concatenate([layer_gains, jnp.stack([d_gf, d_bf])], axis=0)
        grads = grads + micro_grads
    owned = lax.psum_scatter(
        slot_layout(grads, unit_slot, total_slots, rows_unit), "dp", scatter_dimension=0, tiled=True
    )
    gain_grads, loss_sum, loss_count = lax.psum((gain_grads, loss_sum, loss_count), "dp")
    owner_squares = lax.psum(jnp.sum(owned * owned), ("dp", "mp"))
    clip_norm = jnp.sqrt(owner_squares + jnp.sum(gain_grads * gain_grads))
    factor = jnp.minimum(1.0, CLIP_LIMIT / (clip_norm + 1e-06))
    new_master, new_first, new_second = adam_update(
        master, factor * owned, first_moment, second_moment, WEIGHT_DECAY
    )
    new_norms, new_norm_first, new_norm_second = adam_update(
        norm_params, factor * gain_grads, norm_first, norm_second, 0.0
    )
    return (
        new_master,
        new_first,
        new_second,
        new_norms,
        new_norm_first,
        new_norm_second,
        clip_norm,
        loss_sum,
        loss_count,
    )


def solution(mesh):
    placed = (
        P("dp", None),
        P("dp", None),
        P("dp", None),
        P(),
        P("dp", "mp", None),
        P("dp", "mp", None),
        P("dp", "mp", None),
        P(),
        P(),
        P(),
    )
    return jax.shard_map(
        per_device,
        mesh=mesh,
        in_specs=placed,
        out_specs=(
            P("dp", "mp", None),
            P("dp", "mp", None),
            P("dp", "mp", None),
            P(),
            P(),
            P(),
            P(),
            P(),
            P(),
        ),
        check_vma=False,
    )
```

profile of v0, /device:TPU:0, one launch (start us, length us, event | category | flops | bytes accessed | tf_op | source)
XLA Modules:
  0.0 3821.5 jit_solution(2669003335705375882)
XLA Ops:
  16.2 822.4 %all-gather.14.cloned.1.call-done = bf16[336,56,1120]{2,1,0:T(8,128)(2,1)} async-done(((bf16[42,56,1120]{2,1,0:T(8,128)(2,1)}), bf16[336,56,1120]{2,1,0:T(8,128)(2,1)}) %all-gather.14.cloned.1.call-update) | async-done | bytes 42147856 | tf_op jit(solution)/shard_map/all_gather | solution.py:176
  838.6 22.6 gather_fusion
  919.7 86.8 %all-reduce.24.cloned.1.call-done = (f32[512,1120]{0,1:T(8,128)}, f32[512,1120]{0,1:T(8,128)}) async-done(((f32[512,1120]{0,1:T(8,128)}, f32[512,1120]{0,1:T(8,128)}), (f32[512,1120]{0,1:T(8,128)}, f32[512,1120]{0,1:T(8,128)})) %all-reduce.24.cloned.1.call-update) | async-done | bytes 4587536 | tf_op jit(solution)/shard_map/psum | solution.py:57
  1046.1 86.6 %all-reduce.22.cloned.1.call-done = (f32[512,1120]{0,1:T(8,128)}, f32[512,1120]{0,1:T(8,128)}) async-done(((f32[512,1120]{0,1:T(8,128)}, f32[512,1120]{0,1:T(8,128)}), (f32[512,1120]{0,1:T(8,128)}, f32[512,1120]{0,1:T(8,128)})) %all-reduce.22.cloned.1.call-update) | async-done | bytes 4587536 | tf_op jit(solution)/shard_map/psum | solution.py:57
  1156.0 87.5 %all-reduce.20.cloned.1.call-done = (f32[512,1120]{0,1:T(8,128)}, f32[512,1120]{0,1:T(8,128)}) async-done(((f32[512,1120]{0,1:T(8,128)}, f32[512,1120]{0,1:T(8,128)}), (f32[512,1120]{0,1:T(8,128)}, f32[512,1120]{0,1:T(8,128)})) %all-reduce.20.cloned.1.call-update) | async-done | bytes 4587536 | tf_op jit(solution)/shard_map/psum | solution.py:57
  1250.6 23.7 fusion.112
  1300.8 23.0 fusion.111
  1373.1 21.2 fusion.87
  1394.8 30.2 fusion.86
  1425.0 61.7 %all-reduce.18.cloned.1.call-done = (f32[512,1120]{0,1:T(8,128)}, f32[512,1120]{0,1:T(8,128)}) async-done(((f32[512,1120]{0,1:T(8,128)}, f32[512,1120]{0,1:T(8,128)}), (f32[512,1120]{0,1:T(8,128)}, f32[512,1120]{0,1:T(8,128)})) %all-reduce.18.cloned.1.call-update) | async-done | bytes 4587536 | tf_op jit(solution)/shard_map/psum | solution.py:61
  1508.5 30.5 fusion.88
  1539.0 61.7 %all-reduce.16.cloned.1.call-done = (f32[512,1120]{0,1:T(8,128)}, f32[512,1120]{0,1:T(8,128)}) async-done(((f32[512,1120]{0,1:T(8,128)}, f32[512,1120]{0,1:T(8,128)}), (f32[512,1120]{0,1:T(8,128)}, f32[512,1120]{0,1:T(8,128)})) %all-reduce.16.cloned.1.call-update) | async-done | bytes 4587536 | tf_op jit(solution)/shard_map/psum | solution.py:61
  1660.6 70.3 %all-reduce.14.cloned.1.call-done = (f32[512,1120]{0,1:T(8,128)}, f32[512,1120]{0,1:T(8,128)}) async-done(((f32[512,1120]{0,1:T(8,128)}, f32[512,1120]{0,1:T(8,128)}), (f32[512,1120]{0,1:T(8,128)}, f32[512,1120]{0,1:T(8,128)})) %all-reduce.14.cloned.1.call-update) | async-done | bytes 4587536 | tf_op jit(solution)/shard_map/psum | solution.py:61
  1747.0 37.2 scatter_fusion
  1784.2 36.0 scatter_fusion.1
  1820.2 33.1 constant_dynamic-update-slice_fusion
  1853.3 33.1 constant_dynamic-update-slice_fusion.1
  1886.4 61.7 %add.423 = f32[13888,1120]{1,0:T(8,128)} add(f32[13888,1120]{1,0:T(8,128)} %constant_dynamic-update-slice_fusion, f32[13888,1120]{1,0:T(8,128)} %constant_dynamic-update-slice_fusion.1) | non-fusion elementwise | flops 15554560 | bytes 186654720 | tf_op jit(solution)/shard_map/add | solution.py:223
  1948.1 27.0 broadcast_in_dim.51
  1975.1 119.6 %scatter_fusion.2 = f32[336,56,1120]{2,1,0:T(8,128)} fusion(f32[336,56,1120]{2,1,0:T(8,128)} %broadcast_in_dim.51, s32[248]{0:T(256)S(1)} %copy-done.120, f32[248,56,1120]{2,1,0:T(8,128)} %bitcast.217), kind=kCustom, calls=%fused_computation.5 | custom fusion | bytes 186655712 | tf_op jit(solution)/shard_map/scatter | solution.py:138
  2098.0 51.9 %all-reduce = (f32[6,1120]{1,0:T(8,128)S(1)}, f32[]{:T(128)}, f32[]{:T(128)}) all-reduce(f32[6,1120]{1,0:T(8,128)S(1)} %add.425, f32[]{:T(128)S(6)} %add.438, f32[]{:T(128)S(6)} %add.439), channel_id=1, replica_groups=mesh['dp'=8,'mp'=4] {'dp'}, use_global_device_ids=true, to_apply=%region_74.75 | all-reduce | flops 6722 | bytes 53776 | tf_op jit(solution)/shard_map/psum | solution.py:227
  2149.9 1586.3 %reduce-scatter.2.cloned.1.call-done = f32[42,56,1120]{2,1,0:T(8,128)} async-done(((f32[336,56,1120]{2,1,0:T(8,128)}), f32[42,56,1120]{2,1,0:T(8,128)}) %reduce-scatter.2.cloned.1.call-update) | async-done | bytes 10536976 | tf_op jit(solution)/shard_map/reduce_scatter | solution.py:224
  3744.3 39.5 %psum.124 = f32[]{:T(128)} all-reduce(f32[]{:T(128)} %multiply_reduce_fusion), channel_id=1, replica_groups=mesh['dp'=8,'mp'=4] {'dp','mp'}, use_global_device_ids=true, to_apply=%region_61.62 | all-reduce | flops 1 | bytes 8 | tf_op jit(solution)/shard_map/psum | solution.py:228
  3785.9 27.2 multiply_subtract_fusion
  (492 shorter events, 319.5 us)
Async XLA Ops:
  7.2 831.4 %all-gather.14.cloned.1.call-start = ((), (), s32[]{:S(2)}) async-start(), calls=%async_computation.1 | async-start | bytes 48771072 | tf_op jit(solution)/shard_map/all_gather | solution.py:176
  14.3 992.1 %all-reduce.24.cloned.1.call-start = ((), (), s32[]{:S(2)}) async-start(), calls=%async_computation.8 | async-start | bytes 9175040 | tf_op jit(solution)/shard_map/psum | solution.py:57
  16.2 894.6 %copy-start.87 = (f32[1,512]{1,0:T(1,128)}, f32[1,512]{1,0:T(1,128)S(1)}, u32[]{:S(2)}) copy-start(f32[1,512]{1,0:T(1,128)S(1)} %get-tuple-element.501) | copy-start | bytes 6148
  16.2 896.3 %copy-start.85 = (f32[1,512]{1,0:T(1,128)}, f32[1,512]{1,0:T(1,128)S(1)}, u32[]{:S(2)}) copy-start(f32[1,512]{1,0:T(1,128)S(1)} %get-tuple-element.502) | copy-start | bytes 6148
  914.2 218.6 %all-reduce.22.cloned.1.call-start = ((), (), s32[]{:S(2)}) async-start(), calls=%async_computation.7 | async-start | bytes 9175040 | tf_op jit(solution)/shard_map/psum | solution.py:57
  915.5 99.0 %copy-start.51 = (f32[1120]{0:T(1024)}, f32[1120]{0:T(1024)S(1)}, u32[]{:S(2)}) copy-start(f32[1120]{0:T(1024)S(1)} %get-tuple-element.399) | copy-start | bytes 13444
  915.5 99.0 %copy-start.123 = (f32[1120]{0:T(1024)}, f32[1120]{0:T(1024)S(1)}, u32[]{:S(2)}) copy-start(f32[1120]{0:T(1024)S(1)} %get-tuple-element.398) | copy-start | bytes 13444
  915.5 226.5 %copy-start.58 = (f32[1120]{0:T(1024)}, f32[1120]{0:T(1024)S(1)}, u32[]{:S(2)}) copy-start(f32[1120]{0:T(1024)S(1)} %get-tuple-element.397) | copy-start | bytes 13444
  915.5 226.5 %copy-start.121 = (f32[1120]{0:T(1024)}, f32[1120]{0:T(1024)S(1)}, u32[]{:S(2)}) copy-start(f32[1120]{0:T(1024)S(1)} %get-tuple-element.396) | copy-start | bytes 13444
  1040.4 203.1 %all-reduce.20.cloned.1.call-start = ((), (), s32[]{:S(2)}) async-start(), calls=%async_computation.6 | async-start | bytes 9175040 | tf_op jit(solution)/shard_map/psum | solution.py:57
  1151.1 92.4 %copy-start.6 = (f32[512,1120]{0,1:T(8,128)S(1)}, f32[512,1120]{0,1:T(8,128)}, u32[]{:S(2)}) copy-start(f32[512,1120]{0,1:T(8,128)} %copy-done.5) | copy-start | bytes 6881284
  1151.1 335.5 %all-reduce.18.cloned.1.call-start = ((), (), s32[]{:S(2)}) async-start(), calls=%async_computation.5 | async-start | bytes 9175040 | tf_op jit(solution)/shard_map/psum | solution.py:61
  1394.3 92.4 %copy-start.13 = (f32[512,1120]{0,1:T(8,128)S(1)}, f32[512,1120]{0,1:T(8,128)}, u32[]{:S(2)}) copy-start(f32[512,1120]{0,1:T(8,128)} %copy-done.12) | copy-start | bytes 6881284
  1394.3 92.4 %copy-start.84 = (f32[512]{0:T(512)S(1)}, f32[512]{0:T(512)}, u32[]{:S(2)}) copy-start(f32[512]{0:T(512)} %copy-done.83) | copy-start | bytes 6148
  1394.3 206.4 %all-reduce.16.cloned.1.call-start = ((), (), s32[]{:S(2)}) async-start(), calls=%async_computation.4 | async-start | bytes 9175040 | tf_op jit(solution)/shard_map/psum | solution.py:61
  1508.4 92.4 %copy-start.7 = (f32[512,1120]{0,1:T(8,128)S(1)}, f32[512,1120]{0,1:T(8,128)}, u32[]{:S(2)}) copy-start(f32[512,1120]{0,1:T(8,128)} %copy-done.5) | copy-start | bytes 6881284
  1508.4 92.4 %copy-start.59 = (f32[1120]{0:T(1024)S(1)}, f32[1120]{0:T(1024)}, u32[]{:S(2)}) copy-start(f32[1120]{0:T(1024)} %copy-done.58) | copy-start | bytes 13444
  1508.4 222.5 %all-reduce.14.cloned.1.call-start = ((), (), s32[]{:S(2)}) async-start(), calls=%async_computation.3 | async-start | bytes 9175040 | tf_op jit(solution)/shard_map/psum | solution.py:61
  1508.5 97.7 %copy-start.100 = (f32[512]{0:T(512)S(1)}, f32[512]{0:T(512)}, u32[]{:S(2)}) copy-start(f32[512]{0:T(512)} %copy-done.99) | copy-start | bytes 6148
  1508.5 97.7 %copy-start.102 = (f32[512]{0:T(512)S(1)}, f32[512]{0:T(512)}, u32[]{:S(2)}) copy-start(f32[512]{0:T(512)} %copy-done.101) | copy-start | bytes 6148
  1638.5 2097.7 %reduce-scatter.2.cloned.1.call-start = ((), (), s32[]{:S(2)}) async-start(), calls=%async_computation.2 | async-start | bytes 97542144 | tf_op jit(solution)/shard_map/reduce_scatter | solution.py:224
  2149.9 1635.3 %copy-start.54 = (f32[6,1120]{1,0:T(8,128)S(1)}, f32[6,1120]{1,0:T(8,128)}, u32[]{:S(2)}) copy-start(f32[6,1120]{1,0:T(8,128)} %param.21) | copy-start | bytes 80644
  2149.9 1635.3 %copy-start.65 = (f32[6,1120]{1,0:T(8,128)S(1)}, f32[6,1120]{1,0:T(8,128)}, u32[]{:S(2)}) copy-start(f32[6,1120]{1,0:T(8,128)} %param.22) | copy-start | bytes 80644
  2149.9 1635.3 %copy-start.66 = (f32[6,1120]{1,0:T(8,128)S(1)}, f32[6,1120]{1,0:T(8,128)}, u32[]{:S(2)}) copy-start(f32[6,1120]{1,0:T(8,128)} %param.23) | copy-start | bytes 80644
  (129 other events, 1164.5 us)
Sparse Core Ops, SparseCore 0:
  14.4 824.1 all-gather.13
  914.3 92.0 all-reduce.23
  1040.5 92.2 all-reduce.21
  1151.2 92.2 all-reduce.19
  1394.4 92.2 all-reduce.17
  1508.5 92.2 all-reduce.15
  1638.7 92.2 all-reduce.13
  2095.0 1641.1 reduce-scatter.1
where the time goes:
time: 3830 us; the launch traced here: 3820 us
  waiting for transfers between devices  2860 us (75%)
  local copies, waits for them, and re-layouts  319 us (8%)
  other arithmetic  251 us (7%)
  matrix products  241 us (6%)
  blocking collectives  123 us (3%)
    reduce_scatter x1, waiting for transfers between devices, per_device(): lax.psum_scatter(slot_layout(grads, unit_slot, total_slots, rows_unit), '...  1590 us
    all_gather x1, waiting for transfers between devices, per_device(): lax.all_gather(master.astype(jnp.bfloat16), 'dp', axis=0, tiled=True)  822 us
    psum x3, waiting for transfers between devices, branch_sum(): return lax.psum(value, 'mp')  261 us
    psum x3, waiting for transfers between devices, input_sum(): return lax.psum(value, 'mp')  194 us
    scatter x1, local copies, waits for them, and re-layouts, slot_layout(): jnp.zeros((total_slots, rows_unit, grads.shape[1]), jnp.float32)  120 us
    dot_general x10, matrix products, contract_first(): lax.dot_general(left, right, (((0,), (0,)), ((), ())), preferred_element_...  90.4 us
  transfers between devices with their start and end apart: 8, of which 8 were waited for; matrix products, arithmetic and copies ran while one was open for 3% of the time, Pallas kernels for 0%

commit v1 on v0

v1 whole, which is shorter than its diff:
```python
import jax
import jax.numpy as jnp
from jax import lax
from jax.experimental import pallas as pl
from jax.experimental.pallas import tpu as pltpu
from jax.sharding import PartitionSpec as P

HEADS = 20
HD = 56
FF = 4480
V = 42112
STEP = 10


NORM_EPS = 1e-05
LEARN_RATE = 0.1
BETA_ONE = 0.9
BETA_TWO = 0.95
ADAM_EPS = 1e-08
WEIGHT_DECAY = 0.1
CLIP_LIMIT = 1.0
NEG_FILL = -1e30

PICK = 64
F32 = jnp.float32
BF16 = jnp.bfloat16


def dp_pair(value):
    size = lax.axis_size("dp")
    return lax.ppermute(value, "dp", [(d, d ^ 1) for d in range(size)])


def line_hop(value, lane):
    dp, mp = lax.axis_size("dp"), lax.axis_size("mp")
    moves = []
    for d in range(dp):
        for m in range(mp):
            to = d + 2 if (m + lane) % 2 == 0 else d - 2
            if 0 <= to < dp:
                moves.append((d * mp + m, to * mp + m))
    return lax.ppermute(value, ("dp", "mp"), moves)


def dp_flip(value, bit):
    size = lax.axis_size("dp")
    return lax.ppermute(value, "dp", [(d, d ^ bit) for d in range(size)])


def mp_flip(value, bit):
    size = lax.axis_size("mp")
    return lax.ppermute(value, "mp", [(d, d ^ bit) for d in range(size)])


def bits_of(axis):
    return [1 << k for k in range(lax.axis_size(axis).bit_length() - 1)]


def rounded(value):
    return lax.reduce_precision(value, 8, 7)


def half_of(value, which):
    count = value.shape[0] // 2
    return lax.dynamic_slice_in_dim(value, which * count, count, 0)


def in_order(mine, other, which):
    first = jnp.where(which == 0, mine, other)
    second = jnp.where(which == 0, other, mine)
    return jnp.concatenate([first, second], axis=0)


def mp_sum(value, exact=False, stops=()):
    stops = list(stops) + [None] * 3

    def hop(sent, bit, stop):
        got = mp_flip(sent, bit)
        return got if stop is None else stop(got)

    core = lax.axis_index("mp") % 2
    total = half_of(value, core)
    other = half_of(value, 1 - core)
    total = total + hop(other, 1, stops[0])
    for bit in bits_of("mp")[1:]:
        if exact:
            total = total + hop(total, bit, stops[1])
        else:
            total = rounded(total)
            total = total + hop(total.astype(BF16), bit, stops[1]).astype(F32)
    return in_order(total, hop(total, 1, stops[2]), core)


def small_sum(value, axes):
    for axis in axes:
        flip = mp_flip if axis == "mp" else dp_flip
        for bit in bits_of(axis):
            value = value + flip(value, bit)
    return value


def small_gather(value):
    value = value[None]
    me = lax.axis_index("dp")
    for bit in bits_of("dp"):
        value = in_order(value, dp_flip(value, bit), (me // bit) % 2)
    return value


def together(*values):
    return lax.optimization_barrier(values)


def ceil_div(a, b):
    return -((-a) // b)


class Layout:
    def __init__(self, slot, slots, per_line):
        owner = slot // slots
        line = lax.axis_size("dp") // 2
        row, col = owner // 2, owner % 2
        key = (col * line + row) * slots + slot % slots
        me = lax.axis_index("dp")
        rows = jnp.arange(line)
        on_line = (col[:, None] == jnp.arange(2)[None, :])[:, :, None]
        before = on_line & (row[:, None] < rows[None, :])[:, None, :]
        upto = on_line & (row[:, None] <= rows[None, :])[:, None, :]
        self.starts = jnp.sum(before, axis=0).astype(jnp.int32)
        self.ends = jnp.sum(upto, axis=0).astype(jnp.int32)
        self.total = self.ends[:, -1]
        self.base = jnp.zeros((2,), jnp.int32)
        position = jnp.sum(key[None, :] < key[:, None], axis=1).astype(jnp.int32)
        if per_line:
            position = position - jnp.where(col == 1, self.total[0], 0)
        else:
            self.base = self.total[0] * jnp.arange(2)
        self.position, self.col, self.local = position, col, slot % slots
        self.slot, self.count = slot, slot.shape[0]
        self.mine = owner == me
        self.place()

    def place(self):
        me = lax.axis_index("dp")
        z, x = me // 2, me % 2
        self.low, self.other_low = self.base[x], self.base[1 - x]
        self.high, self.other_high = self.low + self.total[x], self.other_low + self.total[1 - x]
        self.first, self.last = self.low + self.starts[x, z], self.low + self.ends[x, z]
        self.longest = jnp.max(self.total)

    def part(self, low, room):
        cut = object.__new__(Layout)
        cut.__dict__.update(self.__dict__)
        cut.starts = jnp.clip(self.starts - low, 0, room)
        cut.ends = jnp.clip(self.ends - low, 0, room)
        cut.total = jnp.clip(self.total - low, 0, room)
        inside = (self.position >= low) & (self.position < low + room)
        cut.position = jnp.where(inside, self.position - low, -1)
        cut.place()
        return cut

    def steps(self, chunk):
        rows = jnp.arange(self.starts.shape[1])
        last = self.starts.shape[1] - 1
        right = ceil_div(self.ends, chunk) + (last - 1 - rows)[None, :]
        left = ceil_div(self.total[:, None] - self.starts, chunk) + (rows - 1)[None, :]
        return jnp.maximum(jnp.max(right[:, :last]), jnp.max(left[:, 1:])).astype(jnp.int32)

    def local_at(self, places):
        hit = (self.position[None, :] == jnp.arange(places)[:, None]) & self.mine[None, :]
        return jnp.sum(jnp.where(hit, self.local[None, :], 0), axis=1)

    def unit_at(self):
        hit = self.position[None, :] == jnp.arange(self.count)[:, None]
        return jnp.sum(jnp.where(hit, jnp.arange(self.count)[None, :], 0), axis=1)

    def at_slot(self, slots):
        hit = self.mine[None, :] & (self.local[None, :] == jnp.arange(slots)[:, None])
        return jnp.sum(jnp.where(hit, self.position[None, :] + 1, 0), axis=1) - 1


def window(store, low, chunk):
    start = jnp.clip(low, 0, store.shape[0] - chunk)
    return start, lax.dynamic_slice_in_dim(store, start, chunk, 0)


def put(store, block, low, valid_low, valid_high, add):
    chunk = block.shape[0]
    start, old = window(store, low, chunk)
    least = jnp.maximum(low, valid_low) - start
    limit = jnp.minimum(low + chunk, valid_high) - start
    place = lax.broadcasted_iota(jnp.int32, block.shape, 0)
    good = (place >= least) & (place < limit)
    if add:
        new = old + jnp.where(good, block.astype(old.dtype), 0)
    else:
        new = jnp.where(good, block, old)
    return lax.dynamic_update_slice_in_dim(store, new, start, 0)


class Stream:
    lanes = 1

    def __init__(self, store, lay, chunk, planned):
        self.store, self.lay, self.chunk, self.planned = store, lay, chunk, planned
        self.needed = jnp.where(lay.longest > 0, self.count_steps(), 0)
        self.done = 0
        self.flight = [None] * self.lanes
        self.prepare()

    def prepare(self):
        pass

    def one(self, store, k):
        blocks = [self.send(self.outgoing(store, k, n), n) for n in range(self.lanes)]
        for n in range(self.lanes):
            store = self.receive(store, blocks[n], k, n)
        return store

    def fly(self, lane, k, value):
        out = self.outgoing(self.store, k, lane)
        self.flight[lane] = self.send(out, lane)
        return value

    def fetch(self, lane, value):
        block = self.flight[lane]
        self.store = self.receive(self.store, block, self.k, lane)
        return value

    def launch(self, value=None):
        self.k = self.order(self.done)
        self.done += 1
        for lane in range(self.lanes):
            value = self.fly(lane, self.k, value)
        return value

    def land(self, value=None):
        for lane in range(self.lanes):
            value = self.fetch(lane, value)
        return value

    def step(self, value=None):
        k = self.order(self.done)
        self.done += 1
        for lane in range(self.lanes):
            value = self.fetch(lane, value)
            value = self.fly(lane, k, value)
        self.k = k
        return value

    def finish(self):
        assert self.done == self.planned
        self.rest()
        return self.store

    def order(self, n):
        return n

    def rest(self):
        self.store = lax.fori_loop(
            self.planned,
            jnp.maximum(self.needed, self.planned),
            lambda k, store: self.one(store, k),
            self.store,
        )


class LineStream(Stream):
    lanes = 2

    def count_steps(self):
        return self.lay.steps(self.chunk)

    def edges(self, k, lane):
        line = lax.axis_size("dp") // 2
        z = lax.axis_index("dp") // 2
        up = (lax.axis_index("mp") + lane) % 2 == 0
        lay, chunk = self.lay, self.chunk
        up_near = lay.low + (k - (line - 2 - z)) * chunk
        down_near = lay.high - (k - z + 2) * chunk
        near = jnp.where(up, up_near, down_near)
        return near, jnp.where(up, up_near - chunk, down_near + chunk), up


class Spread(LineStream):
    def prepare(self):
        self.store = lax.fori_loop(
            0,
            jnp.maximum(self.needed - self.planned, 0),
            lambda i, store: self.one(store, self.needed - 1 - i),
            self.store,
        )

    def order(self, n):
        return self.planned - 1 - n

    def rest(self):
        pass

    def outgoing(self, store, k, lane):
        return window(store, self.edges(k, lane)[0], self.chunk)[1]

    def send(self, out, lane):
        return line_hop(out, lane)

    def receive(self, store, block, k, lane):
        _, far, up = self.edges(k, lane)
        low = jnp.where(up, self.lay.low, self.lay.last)
        high = jnp.where(up, self.lay.first, self.lay.high)
        return put(store, block, far, low, high, False)


class Collect(LineStream):
    def outgoing(self, store, k, lane):
        return window(store, self.edges(k, lane)[1], self.chunk)[1].astype(BF16)

    def send(self, out, lane):
        return line_hop(out, 1 - lane)

    def receive(self, store, block, k, lane):
        near, _, up = self.edges(k, lane)
        low = jnp.where(up, self.lay.low, self.lay.first)
        high = jnp.where(up, self.lay.last, self.lay.high)
        return put(store, block, near, low, high, True)


class PairStream(Stream):
    def count_steps(self):
        return ceil_div(self.lay.longest, self.chunk)

    def send(self, out, lane):
        return dp_pair(out)


class Swap(PairStream):
    def outgoing(self, store, k, lane):
        return window(store, self.lay.low + k * self.chunk, self.chunk)[1]

    def receive(self, store, block, k, lane):
        lay = self.lay
        low = lay.other_low + k * self.chunk
        return put(store, block, low, lay.other_low, lay.other_high, False)


class Fold(PairStream):
    def outgoing(self, store, k, lane):
        low = self.lay.other_low + k * self.chunk
        return window(store, low, self.chunk)[1].astype(BF16)

    def receive(self, store, block, k, lane):
        lay = self.lay
        return put(store, block, lay.low + k * self.chunk, lay.low, lay.high, True)


def layer_norm(x, gain, shift):
    centred = x - jnp.mean(x, axis=-1, keepdims=True)
    scale = lax.rsqrt(jnp.mean(centred * centred, axis=-1, keepdims=True) + NORM_EPS)
    return centred * scale * gain + shift


def segment_ids(lengths, span):
    bounds = jnp.cumsum(lengths, axis=-1)
    return jnp.sum(jnp.arange(span)[None, :, None] >= bounds[:, None, :], axis=-1)


def dot_t(left, right):
    return lax.dot_general(left, right, (((1,), (1,)), ((), ())), preferred_element_type=F32)


def dot_first(left, right):
    return lax.dot_general(left, right, (((0,), (0,)), ((), ())), preferred_element_type=F32)


def dot_plain(left, right):
    return jnp.dot(left, right, preferred_element_type=F32)


def attention_probs(query, keys, seg):
    span = seg.shape[1]
    scores = jnp.einsum("bqhd,bkhd->bhqk", query, keys, preferred_element_type=F32) * HD ** (-0.5)
    place = jnp.arange(span)
    allowed = (seg[:, :, None] == seg[:, None, :]) & (place[None, None, :] <= place[None, :, None])
    scores = jnp.where(allowed[:, None], scores, NEG_FILL)
    expo = jnp.exp(scores - jnp.max(scores, axis=-1, keepdims=True))
    return expo / jnp.sum(expo, axis=-1, keepdims=True)


def assemble_kernel(kind_ref, e_at, f_at, a_at, rows_ref, e_ref, f_ref, a_ref, out_ref, sq_ref):
    slot = pl.program_id(0)
    kind = kind_ref[slot]
    value = jnp.where(kind == 0, e_ref[...], 0.0)
    value = jnp.where(kind == 1, f_ref[...], value)
    value = rows_ref[...] + jnp.where(kind == 2, a_ref[...], value)
    out_ref[...] = value

    @pl.when(slot == 0)
    def _():
        sq_ref[...] = jnp.zeros(sq_ref.shape, F32)

    _, rows, width = value.shape
    sq_ref[...] += jnp.sum((value * value).reshape(rows // 8, 8, width), axis=0)


def assemble(rows, grads, index):
    slots, rows_unit, width = rows.shape
    kind = jnp.full((slots,), 3, jnp.int32)
    for number, at in enumerate(index):
        kind = jnp.where(at >= 0, number, kind)
    index = [jnp.maximum(at, 0).astype(jnp.int32) for at in index]
    block = (1, rows_unit, width)
    return pl.pallas_call(
        assemble_kernel,
        grid_spec=pltpu.PrefetchScalarGridSpec(
            num_scalar_prefetch=4,
            grid=(slots,),
            in_specs=[
                pl.BlockSpec(block, lambda s, k, e, f, a: (s, 0, 0)),
                pl.BlockSpec(block, lambda s, k, e, f, a: (e[s], 0, 0)),
                pl.BlockSpec(block, lambda s, k, e, f, a: (f[s], 0, 0)),
                pl.BlockSpec(block, lambda s, k, e, f, a: (a[s], 0, 0)),
            ],
            out_specs=[
                pl.BlockSpec(block, lambda s, k, e, f, a: (s, 0, 0)),
                pl.BlockSpec((8, width), lambda s, k, e, f, a: (0, 0)),
            ],
        ),
        out_shape=[
            jax.ShapeDtypeStruct(rows.shape, F32),
            jax.ShapeDtypeStruct((8, width), F32),
        ],
    )(kind, *index, rows, *grads)


def when(wanted, work, value, *given):
    def turn(i, so_far):
        i, *held = together(i, *given)
        return work(so_far, *held)

    return lax.fori_loop(0, wanted.astype(jnp.int32), turn, value)


def adam_update(weight, grad, first, second, decay):
    first = BETA_ONE * first + (1.0 - BETA_ONE) * grad
    second = BETA_TWO * second + (1.0 - BETA_TWO) * grad * grad
    stride = first / (1.0 - BETA_ONE**STEP) / (jnp.sqrt(second / (1.0 - BETA_TWO**STEP)) + ADAM_EPS)
    return (weight - LEARN_RATE * (stride + decay * weight), first, second)


def merge_stats(left, right):
    top = jnp.maximum(left[0], right[0])
    total = left[1] * jnp.exp(left[0] - top) + right[1] * jnp.exp(right[0] - top)
    return jnp.stack([top, total, left[2] + right[2]])


def per_device(
    token_ids,
    seg_lengths,
    counted,
    unit_slot,
    master,
    first_moment,
    second_moment,
    norm_params,
    norm_first,
    norm_second,
):
    slots, rows_unit, width = master.shape
    dp = lax.axis_size("dp")
    parts = lax.axis_size("mp")
    me = lax.axis_index("dp")
    piece = lax.axis_index("mp")
    heads = HEADS // parts
    q_rows = heads * HD
    ff_rows = FF // parts
    vocab_rows = V // parts
    a_units = 4 * q_rows // rows_unit
    f_units = 2 * ff_rows // rows_unit
    e_units = vocab_rows // rows_unit
    packs, span = token_ids.shape
    tokens = packs * span
    root = width**0.5
    line = dp // 2

    a_end, f_end = a_units, a_units + f_units
    lay_a = Layout(unit_slot[:a_end], slots, False)
    lay_f = Layout(unit_slot[a_end:f_end], slots, False)
    lay_e = Layout(unit_slot[f_end:], slots, True)
    most = min(e_units, line * slots)
    usual = min(most, 112)
    crowded = lay_e.longest > usual
    lay_m = lay_e.part(0, usual)
    lay_t = lay_e.part(usual, most - usual) if most > usual else None

    own = master.astype(BF16)

    at_a, at_f, at_e = lay_a.local_at(a_units), lay_f.local_at(f_units), lay_m.local_at(usual)
    spread_a = Spread(master[at_a].astype(BF16), lay_a, 5, 3)
    at_f = spread_a.launch(at_f)
    spread_f = Spread(own[at_f], lay_f, 9, 3)
    at_e = spread_f.launch(at_e)
    spread_e = Spread(own[at_e], lay_m, 21, 4)
    spread_e.launch()
    packed = small_gather(jnp.concatenate([token_ids, seg_lengths, counted], axis=1))

    ids_all = packed[:, :, :span].reshape(dp, tokens)
    piece_all = ids_all // vocab_rows
    local_all = ids_all % vocab_rows
    block_all = local_all // rows_unit
    hit = block_all[:, :, None] == jnp.arange(e_units)[None, None, :]
    slot_all = jnp.sum(jnp.where(hit, lay_e.slot[None, None, :], 0), axis=-1)
    code_all = piece_all * dp + slot_all // slots
    code_all = spread_f.step(spread_a.step(code_all))
    order = jnp.arange(tokens)
    earlier = order[None, None, :] < order[None, :, None]
    repeat = jnp.any((ids_all[:, :, None] == ids_all[:, None, :]) & earlier, axis=-1)
    first_all = ~repeat
    first_all = spread_e.step(first_all)
    rank_all = jnp.sum(
        (code_all[:, :, None] == code_all[:, None, :]) & earlier & first_all[:, None, :],
        axis=-1,
    ).astype(jnp.int32)
    rank_all = spread_f.step(spread_a.step(rank_all))
    rounds = jnp.max(jnp.where(first_all, rank_all, 0)) // PICK + 1
    mine_all = first_all & (code_all == piece * dp + me)
    row_all = (slot_all % slots) * rows_unit + local_all % rows_unit
    ids_own = token_ids.reshape(tokens)

    def own_view(array, which=me):
        return lax.dynamic_index_in_dim(array, which, 0, False)

    code_own = own_view(code_all)
    same = (ids_own[:, None] == ids_own[None, :]) & own_view(first_all)[None, :]
    rank_own = jnp.sum(jnp.where(same, own_view(rank_all)[None, :], 0), axis=-1)
    inside_own = (code_own // dp) == piece
    owner_own = code_own % dp

    def owner_picks(turn):
        wanted = turn * PICK + jnp.arange(PICK)
        hit = mine_all[:, None, :] & (rank_all[:, None, :] == wanted[None, :, None])
        row = jnp.sum(jnp.where(hit, row_all[:, None, :] + 1, 0), axis=-1) - 1
        row = row.reshape(dp * PICK)
        return (row[:, None] == jnp.arange(slots * rows_unit)[None, :]).astype(BF16)

    def token_picks(turn):
        rank = rank_own - turn * PICK
        good = inside_own & (rank >= 0) & (rank < PICK)
        key = jnp.where(good, owner_own * PICK + rank, -1)
        return (key[:, None] == jnp.arange(dp * PICK)[None, :]).astype(BF16)

    def find(turn):
        rows = dot_plain(owner_picks(turn), own.reshape(slots * rows_unit, width)).astype(BF16)
        return lax.all_to_all(rows.reshape(dp, PICK, width), "dp", 0, 0)

    def fill_in(turn, rows):
        return dot_plain(token_picks(turn), rows.reshape(dp * PICK, width)).astype(BF16)

    x0 = fill_in(0, find(0))
    x0 = lax.fori_loop(1, rounds, lambda i, t: t + fill_in(i, find(i)), x0)
    x0 = spread_e.step(x0)
    x0 = mp_sum(x0, True)
    x0 = spread_a.land(x0)
    swap_a = Swap(spread_a.finish(), lay_a, 13, 1)
    x0 = swap_a.launch(x0)
    x0 = spread_f.land(x0)
    swap_f = Swap(spread_f.finish(), lay_f, 26, 1)
    x0 = swap_f.launch(x0).astype(F32) * root

    gains = norm_params
    seg = segment_ids(seg_lengths, span)
    a1b = layer_norm(x0, gains[0], gains[1]).astype(BF16)
    a1b = swap_a.land(a1b)
    w_a = swap_a.finish()[lay_a.position].reshape(a_units * rows_unit, width)
    w_qkv, w_out = w_a[: 3 * q_rows], w_a[3 * q_rows :]
    qkv = dot_t(a1b, w_qkv).astype(BF16).reshape(packs, span, 3, heads, HD)
    qkv = spread_e.step(qkv)
    query, keys, values = qkv[:, :, 0], qkv[:, :, 1], qkv[:, :, 2]
    probs = attention_probs(query, keys, seg)
    mixed = jnp.einsum("bhqk,bkhd->bqhd", probs.astype(BF16), values, preferred_element_type=F32)
    mixed = mixed.reshape(tokens, heads * HD).astype(BF16)

    def stop_f(got):
        got = swap_f.land(got)
        later["f"] = swap_f.finish()[lay_f.position].reshape(f_units * rows_unit, width)
        return got

    later = {}
    x1 = x0 + mp_sum(dot_plain(mixed, w_out), False, (None, stop_f))
    w_up, w_down = later["f"][:ff_rows], later["f"][ff_rows:]
    x1 = spread_e.land(x1)
    table = spread_e.finish().reshape(usual * rows_unit, width)
    a2b = layer_norm(x1, gains[2], gains[3]).astype(BF16)
    pre = dot_t(a2b, w_up)
    hidden = jax.nn.gelu(pre).astype(BF16)
    x2 = x1 + mp_sum(dot_plain(hidden, w_down))
    final_low = layer_norm(x2, gains[4], gains[5]).astype(BF16)

    core = piece % 2
    theirs = dp_pair(half_of(final_low, core))
    theirs = in_order(theirs, mp_flip(theirs, 1), core)
    both = jnp.concatenate([final_low, theirs], axis=0)
    pair_data = jnp.stack([own_view(packed), own_view(packed, me ^ 1)])
    pair_ids = pair_data[:, :, :span]
    pair_lengths = pair_data[:, :, span : span + seg_lengths.shape[1]]
    pair_seg = segment_ids(pair_lengths.reshape(2 * packs, -1), span).reshape(2, packs, span)
    pair_counted = pair_data[:, :, span + seg_lengths.shape[1] :]
    counts = (pair_seg[:, :, 1:] == pair_seg[:, :, :-1]) & (pair_counted[:, :, :-1] == 1)
    keep = jnp.concatenate([counts, jnp.zeros((2, packs, 1), bool)], axis=2)
    keep = keep.astype(F32).reshape(2 * tokens)
    target = jnp.concatenate([pair_ids[:, :, 1:], pair_ids[:, :, :1]], axis=2)
    target = target.reshape(2 * tokens)
    t_local = target % vocab_rows
    here = (lay_e.col == me % 2)[None, :] & (
        (t_local // rows_unit)[:, None] == jnp.arange(e_units)[None, :]
    )
    t_block = jnp.sum(jnp.where(here, lay_e.position[None, :] + 1, 0), axis=1) - 1
    t_row = t_block * rows_unit + t_local % rows_unit
    t_row = jnp.where((target // vocab_rows == piece) & (t_block >= 0), t_row, -1)

    def scores(table, lay, low, both):
        place = jnp.arange(table.shape[0])
        real = (place < lay.high * rows_unit)[None, :]
        onehot = (place + low * rows_unit)[None, :] == t_row[:, None]
        return dot_t(both, table), real, onehot

    def measures(logits, real, onehot):
        top = jnp.max(jnp.where(real, logits, NEG_FILL), axis=-1)
        total = jnp.sum(jnp.where(real, jnp.exp(logits - top[:, None]), 0.0), axis=-1)
        picked = jnp.sum(jnp.where(onehot, logits, 0.0), axis=-1)
        return jnp.stack([top, total, picked])

    def slopes(logits, real, onehot, lse):
        prob = jnp.where(real, jnp.exp(logits - lse[:, None]), 0.0)
        return (keep[:, None] * (prob - onehot.astype(F32))).astype(BF16)

    logits, real, onehot = scores(table, lay_m, 0, both)
    stats = measures(logits, real, onehot)
    if lay_t is not None:

        def spill(own):
            stream = Spread(own[lay_t.local_at(most - usual)], lay_t, 8, 0)
            return stream.store.reshape(-1, width)

        def more_stats(stats, own, both):
            return merge_stats(stats, measures(*scores(spill(own), lay_t, usual, both)))

        stats = when(crowded, more_stats, stats, own, both)
    for bit in bits_of("mp"):
        stats = merge_stats(stats, mp_flip(stats, bit))
    their_stats = dp_pair(stats)
    their_stats = jnp.concatenate([their_stats[:, tokens:], their_stats[:, :tokens]], axis=1)
    stats = merge_stats(stats, their_stats)
    lse = stats[0] + jnp.log(stats[1])
    loss_sum = jnp.sum((keep * (lse - stats[2]))[:tokens])
    loss_count = jnp.sum(keep[:tokens])
    d_logits = slopes(logits, real, onehot, lse)
    half = tokens // 2

    def halved(total):
        total = total.reshape(2, tokens, width)
        sent = lax.dynamic_slice_in_dim(total, (1 - core) * half, half, 1)
        kept = lax.dynamic_slice_in_dim(total, core * half, half, 1)
        return kept, sent

    part, sent = halved(dot_plain(d_logits, table))
    d_logits, sent = together(d_logits, sent)
    swapped = mp_flip(sent, 1)
    grad_e = dot_first(d_logits, both).reshape(usual, rows_unit, width)
    part = part + swapped
    collect_e = Collect(grad_e, lay_m, 21, 4)
    collect_e.launch()
    part = part[0] + dp_pair(part[1].astype(BF16)).astype(F32)
    if lay_t is not None:

        def more_final(total, own, both, lse):
            rest = spill(own)
            slope = slopes(*scores(rest, lay_t, usual, both), lse)
            kept, sent = halved(dot_plain(slope, rest))
            kept = kept + mp_flip(sent, 1)
            return total + kept[0] + dp_pair(kept[1].astype(BF16)).astype(F32)

        part = part + when(crowded, more_final, jnp.zeros(part.shape, F32), own, both, lse)
    for bit in bits_of("mp")[1:]:
        part = rounded(part)
        part = part + collect_e.step(mp_flip(part.astype(BF16), bit)).astype(F32)
    d_final = in_order(part, mp_flip(part, 1), core)

    dx2, d_gf, d_bf = jax.vjp(layer_norm, x2, gains[4], gains[5])[1](d_final)
    dz = dx2.astype(BF16)
    d_hidden = dot_t(dz, w_down)
    d_pre = jax.vjp(jax.nn.gelu, pre)[1](d_hidden)[0].astype(BF16)

    def blocks_in_order(lay, parts):
        grad = jnp.concatenate(parts, axis=0).reshape(lay.count, rows_unit, width)
        return grad[lay.unit_at()]

    d_a2 = mp_sum(dot_plain(d_pre, w_up), False, (None, collect_e.step))
    grad_f = blocks_in_order(lay_f, [dot_first(d_pre, a2b), dot_first(hidden, dz)])
    fold_f = Fold(grad_f, lay_f, 26, 1)
    d_a2 = fold_f.launch(d_a2)
    dx1_norm, d_g2, d_b2 = jax.vjp(layer_norm, x1, gains[2], gains[3])[1](d_a2)
    dx1 = dx2 + dx1_norm
    dy = dx1.astype(BF16)
    d_mixed = dot_t(dy, w_out).astype(BF16).reshape(packs, span, heads, HD)
    d_probs = jnp.einsum("bqhd,bkhd->bhqk", d_mixed, values, preferred_element_type=F32)
    d_values = jnp.einsum(
        "bhqk,bqhd->bkhd", probs.astype(BF16), d_mixed, preferred_element_type=F32
    )
    d_probs = collect_e.step(d_probs)
    d_scores = (probs * (d_probs - jnp.sum(probs * d_probs, axis=-1, keepdims=True))).astype(BF16)
    d_query = jnp.einsum("bhqk,bkhd->bqhd", d_scores, keys, preferred_element_type=F32)
    d_keys = jnp.einsum("bhqk,bqhd->bkhd", d_scores, query, preferred_element_type=F32)
    d_query, d_keys = d_query * HD ** (-0.5), d_keys * HD ** (-0.5)
    d_qkv = jnp.stack([d_query, d_keys, d_values], axis=2)
    d_qkv = d_qkv.reshape(tokens, 3 * heads * HD).astype(BF16)

    d_a1 = dot_plain(d_qkv, w_qkv)
    grad_a = blocks_in_order(lay_a, [dot_first(d_qkv, a1b), dot_first(mixed, dy)])
    fold_a = Fold(grad_a, lay_a, 13, 1)
    fold_a.launch()

    def stop_e(got):
        got = fold_f.land(collect_e.land(got))
        later["f"] = Collect(fold_f.finish(), lay_f, 9, 3)
        return later["f"].launch(got)

    d_a1 = mp_sum(d_a1, False, (stop_e, None, lambda got: later["f"].step(got)))
    grad_e, collect_f = collect_e.finish(), later["f"]
    d_a1 = fold_a.land(d_a1)
    collect_a = Collect(fold_a.finish(), lay_a, 5, 3)
    d_a1 = collect_a.launch(d_a1)
    dx0_norm, d_g1, d_b1 = jax.vjp(layer_norm, x0, gains[0], gains[1])[1](d_a1)
    dx0 = dx1 + dx0_norm
    d_rows = dx0 * root
    d_high = rounded(d_rows)
    d_low = (d_rows - d_high).astype(BF16)
    d_high = d_high.astype(BF16)

    def give(turn):
        picks = token_picks(turn)
        rows = (dot_first(picks, d_high) + dot_first(picks, d_low)).astype(BF16)
        return lax.all_to_all(rows.reshape(dp, PICK, width), "dp", 0, 0)

    def take(turn, rows):
        return dot_first(owner_picks(turn), rows.reshape(dp * PICK, width))

    rows = collect_a.step(collect_f.step(give(0)))
    owned = take(0, rows)
    owned = lax.fori_loop(1, rounds, lambda i, t: t + take(i, give(i)), owned)
    owned = owned.reshape(slots, rows_unit, width)
    owned = collect_a.step(owned)
    if lay_t is not None:

        def more_owned(owned, own, both, lse):
            grad = dot_first(slopes(*scores(spill(own), lay_t, usual, both), lse), both)
            stream = Collect(grad.reshape(-1, rows_unit, width), lay_t, 8, 0)
            stream.rest()
            index = lay_t.at_slot(slots)
            block = stream.store[jnp.maximum(index, 0)]
            return owned + jnp.where((index >= 0)[:, None, None], block, 0.0)

        owned = when(crowded, more_owned, owned, own, both, lse)
    owned = collect_a.land(collect_f.land(owned))
    grad_f, grad_a = collect_f.finish(), collect_a.finish()
    index = [lay.at_slot(slots) for lay in (lay_m, lay_f, lay_a)]
    owned, squares = assemble(owned, (grad_e, grad_f, grad_a), index)

    owner_squares = small_sum(jnp.sum(squares), ("mp",))
    sums = jnp.stack([loss_sum, loss_count, owner_squares] + [jnp.zeros(())] * (width - 3))
    sums = small_sum(jnp.stack([d_g1, d_b1, d_g2, d_b2, d_gf, d_bf, sums, sums]), ("dp",))
    gain_grads, loss_sum, loss_count, owner_squares = sums[:6], sums[6, 0], sums[6, 1], sums[6, 2]
    clip_norm = jnp.sqrt(owner_squares + jnp.sum(gain_grads * gain_grads))
    factor = jnp.minimum(1.0, CLIP_LIMIT / (clip_norm + 1e-06))
    new_master, new_first, new_second = adam_update(
        master, factor * owned, first_moment, second_moment, WEIGHT_DECAY
    )
    new_norms, new_norm_first, new_norm_second = adam_update(
        norm_params, factor * gain_grads, norm_first, norm_second, 0.0
    )
    return (
        new_master,
        new_first,
        new_second,
        new_norms,
        new_norm_first,
        new_norm_second,
        clip_norm,
        loss_sum,
        loss_count,
    )


def solution(mesh):
    placed = (
        P("dp", None),
        P("dp", None),
        P("dp", None),
        P(),
        P("dp", "mp", None),
        P("dp", "mp", None),
        P("dp", "mp", None),
        P(),
        P(),
        P(),
    )
    return jax.shard_map(
        per_device,
        mesh=mesh,
        in_specs=placed,
        out_specs=(
            P("dp", "mp", None),
            P("dp", "mp", None),
            P("dp", "mp", None),
            P(),
            P(),
            P(),
            P(),
            P(),
            P(),
        ),
        check_vma=False,
    )
```

time: 3830 us -> 1470 us (0.38)
  waiting for transfers between devices: 2860 us -> 337 us
  starting transfers between devices: 1.58 us -> 193 us
  other arithmetic: 251 us -> 414 us
  blocking collectives: 123 us -> 0 us
  local copies, waits for them, and re-layouts: 319 us -> 197 us
    reduce_scatter x1 -> x0, waiting for transfers between devices: 1590 us -> none  [per_device(): lax.psum_scatter(slot_layout(grads, unit_slot, total_slots, rows_unit), '...]
    all_gather x1 -> x0, waiting for transfers between devices: 822 us -> none  [per_device(): lax.all_gather(master.astype(jnp.bfloat16), 'dp', axis=0, tiled=True)]
    psum x6 -> x0, waiting for transfers between devices: 455 us -> none  [the longest x3 261 us: branch_sum(): return lax.psum(value, 'mp')]
    ppermute x0 -> x76, waiting for transfers between devices: none -> 337 us  [the longest x40 200 us: line_hop(): return lax.ppermute(value, ('dp', 'mp'), moves)]
    ppermute x0 -> x76, starting transfers between devices: none -> 184 us  [the longest x40 131 us: line_hop(): return lax.ppermute(value, ('dp', 'mp'), moves)]
    scatter x1 -> x0, local copies, waits for them, and re-layouts: 120 us -> none  [slot_layout(): jnp.zeros((total_slots, rows_unit, grads.shape[1]), jnp.float32)]
    dynamic_update_slice x0 -> x27, other arithmetic: none -> 115 us  [put(): return lax.dynamic_update_slice_in_dim(store, new, start, 0)]
    psum x2 -> x0, blocking collectives: 91.4 us -> none  [the longest x1 51.9 us: per_device(): lax.psum((gain_grads, loss_sum, loss_count), 'dp')]
  transfers between devices with their start and end apart: 8 -> 78, of which waited for: 8 -> 33; matrix products, arithmetic and copies ran while one was open for 3% -> 41% of each run, Pallas kernels for 0% -> 0%
where the time goes in v1:
time: 1470 us; the launch traced here: 1460 us
  other arithmetic  414 us (28%)
  waiting for transfers between devices  337 us (23%)
  matrix products  207 us (14%)
  local copies, waits for them, and re-layouts  197 us (13%)
  starting transfers between devices  193 us (13%)
  between operations  58.9 us (4%)
  Pallas kernels  30.2 us (2%)
  loops' own time  19.4 us (1%)
    ppermute x40, waiting for transfers between devices, line_hop(): return lax.ppermute(value, ('dp', 'mp'), moves)  200 us
    ppermute x40, starting transfers between devices, line_hop(): return lax.ppermute(value, ('dp', 'mp'), moves)  131 us
    dynamic_update_slice x27, other arithmetic, put(): return lax.dynamic_update_slice_in_dim(store, new, start, 0)  115 us
    ppermute x7, waiting for transfers between devices, dp_pair(): return lax.ppermute(value, 'dp', [(d, d ^ 1) for d in range(size)])  99.1 us
    dynamic_slice x17, other arithmetic, window(): return (start, lax.dynamic_slice_in_dim(store, start, chunk, 0))  74.3 us
    dot_general x8, matrix products, dot_first(): lax.dot_general(left, right, (((0,), (0,)), ((), ())), preferred_element_...  65.1 us
    dot_general x7, matrix products, dot_plain(): return jnp.dot(left, right, preferred_element_type=F32)  64.4 us
    convert_element_type x17, local copies, waits for them, and re-layouts, outgoing(): return window(store, self.edges(k, lane)[1], self.chunk)[1].astype(BF16)  55.5 us
  transfers between devices with their start and end apart: 78, of which 33 were waited for; matrix products, arithmetic and copies ran while one was open for 41% of the time, Pallas kernels for 0%

profile of v1, /device:TPU:0, one launch (start us, length us, event | category | flops | bytes accessed | tf_op | source)
XLA Modules:
  0.0 1456.5 jit_solution(1711683748776706781)
XLA Ops:
  23.5 10.1 gather_fusion.8
  120.8 9.8 convert_reduce_fusion
  164.9 18.3 %collective-permute-done.34 = bf16[5,56,1120]{2,1,0:T(8,128)(2,1)} collective-permute-done((bf16[5,56,1120]{2,1,0:T(8,128)(2,1)}, bf16[5,56,1120]{2,1,0:T(8,128)(2,1)}, u32[]{:S(2)}, u32[]{:S(2)}) %collective-permute-start.34) | collective-permute-done | bytes 627232 | tf_op jit(solution)/shard_map/ppermute | solution.py:42
  225.9 12.9 collective-permute-done.44
  376.5 31.0 %collective-permute-done.48 = bf16[26,56,1120]{2,1,0:T(8,128)(2,1)} collective-permute-done((bf16[26,56,1120]{2,1,0:T(8,128)(2,1)}, bf16[26,56,1120]{2,1,0:T(8,128)(2,1)}, u32[]{:S(2)}, u32[]{:S(2)}) %collective-permute-start.48) | collective-permute-done | bytes 3261472 | tf_op jit(solution)/shard_map/ppermute | solution.py:31
  472.2 11.4 collective-permute-done.58
  543.6 22.9 %collective-permute-done.60 = bf16[21,56,1120]{2,1,0:T(8,128)(2,1)S(1)} collective-permute-done((bf16[21,56,1120]{2,1,0:T(8,128)(2,1)S(1)}, bf16[21,56,1120]{2,1,0:T(8,128)(2,1)S(1)}, u32[]{:S(2)}, u32[]{:S(2)}) %collective-permute-start.60) | collective-permute-done | bytes 2634272 | tf_op jit(solution)/shard_map/ppermute | solution.py:42
  591.1 16.7 %collective-permute-done.61 = bf16[21,56,1120]{2,1,0:T(8,128)(2,1)} collective-permute-done((bf16[21,56,1120]{2,1,0:T(8,128)(2,1)}, bf16[21,56,1120]{2,1,0:T(8,128)(2,1)}, u32[]{:S(2)}, u32[]{:S(2)}) %collective-permute-start.61) | collective-permute-done | bytes 2634272 | tf_op jit(solution)/shard_map/ppermute | solution.py:42
  612.8 41.4 %select_reduce_fusion.11 = (f32[2048]{0:T(1024)S(1)}, f32[2048,6272]{1,0:T(8,128)}) fusion(pred[6272]{0:T(1024)(128)(4,1)S(1)} %iota_compare_fusion.36, bf16[6272,1120]{1,0:T(8,128)(2,1)} %bitcast.64, bf16[512,1120]{0,1:T(8,128)(2,1)S(1)} %copy-done.37, bf16[512,1120]{0,1:T(8,128)(2,1)S(1)} %get-tuple-element.3999, bf16[1024,1120]{0,1:T(8,128)(2,1)S(1)} %add_convert_fusion), kind=kOutput, calls=%fused_computation.168 | convolution fusion | flops 28812376064 | bytes 70031488 | tf_op jit(solution)/shard_map/dot_general | solution.py:367
  654.1 18.1 %select_reduce_fusion.10 = (f32[2048]{0:T(1024)S(1)}, f32[2048]{0:T(1024)S(1)}) fusion(f32[2048,6272]{1,0:T(8,128)} %get-tuple-element.4084, f32[2048]{0:T(1024)S(1)} %get-tuple-element.4083, pred[6272]{0:T(1024)(128)(4,1)S(1)} %iota_compare_fusion.36, s32[2048]{0:T(1024)S(1)} %fusion.110), kind=kLoop, calls=%fused_computation.167 | loop fusion | flops 77066240 | bytes 51419264 | tf_op jit(solution)/shard_map/reduce_sum | solution.py:627
  682.9 26.6 %multiply_convert_fusion.2 = bf16[2048,6272]{1,0:T(8,128)(2,1)} fusion(f32[2048,6272]{1,0:T(8,128)} %get-tuple-element.4084, f32[2048]{0:T(1024)S(1)} %log_add_fusion, s32[2048]{0:T(1024)} %copy-done.67, f32[2048]{0:T(1024)S(1)} %bitcast.400, pred[6272]{0:T(1024)(128)(4,1)S(1)} %copy-done.106), kind=kLoop, calls=%fused_computation.164 | loop fusion | flops 89915392 | bytes 77101184 | tf_op jit(solution)/shard_map/convert_element_type | solution.py:633
  709.5 41.1 %fusion.177 = f32[2,1024,1120]{1,2,0:T(8,128)S(1)} fusion(bf16[2,1024,6272]{2,1,0:T(8,128)(2,1)} %bitcast.363, bf16[6272,1120,1]{1,0,2:T(8,128)(2,1)} %bitcast.80), kind=kOutput, calls=%fused_computation.789 | convolution fusion | flops 28772925440 | bytes 48914432 | tf_op jit(solution)/shard_map/dot_general | solution.py:375
  752.8 39.4 %fusion.149 = f32[6272,1120]{1,0:T(8,128)} fusion(bf16[2048,6272]{1,0:T(8,128)(2,1)} %multiply_convert_fusion.2, bf16[512,1120]{0,1:T(8,128)(2,1)S(1)} %copy-done.38, bf16[512,1120]{0,1:T(8,128)(2,1)S(1)} %copy-done.35, bf16[1024,1120]{0,1:T(8,128)(2,1)S(1)} %copy-done.20), kind=kOutput, calls=%fused_computation.767 | convolution fusion | flops 28786688000 | bytes 58376192 | tf_op jit(solution)/shard_map/dot_general | solution.py:371
  816.1 22.9 %collective-permute-done.66 = bf16[512,1120]{0,1:T(8,128)(2,1)} collective-permute-done((bf16[512,1120]{0,1:T(8,128)(2,1)}, bf16[512,1120]{0,1:T(8,128)(2,1)}, u32[]{:S(2)}, u32[]{:S(2)}) %collective-permute-start.66) | collective-permute-done | bytes 1146912 | tf_op jit(solution)/shard_map/ppermute | solution.py:31
  845.0 14.8 %collective-permute-done.75 = bf16[21,56,1120]{2,1,0:T(8,128)(2,1)} collective-permute-done((bf16[21,56,1120]{2,1,0:T(8,128)(2,1)}, bf16[21,56,1120]{2,1,0:T(8,128)(2,1)}, u32[]{:S(2)}, u32[]{:S(2)}) %collective-permute-start.75) | collective-permute-done | bytes 2634272 | tf_op jit(solution)/shard_map/ppermute | solution.py:42
  894.3 24.0 %collective-permute-done.77 = bf16[21,56,1120]{2,1,0:T(8,128)(2,1)} collective-permute-done((bf16[21,56,1120]{2,1,0:T(8,128)(2,1)}, bf16[21,56,1120]{2,1,0:T(8,128)(2,1)}, u32[]{:S(2)}, u32[]{:S(2)}) %collective-permute-start.77) | collective-permute-done | bytes 2634272 | tf_op jit(solution)/shard_map/ppermute | solution.py:42
  960.9 11.6 gather_fusion.9
  1014.8 29.8 %collective-permute-done.83 = bf16[26,56,1120]{2,1,0:T(8,128)(2,1)S(1)} collective-permute-done((bf16[26,56,1120]{2,1,0:T(8,128)(2,1)S(1)}, bf16[26,56,1120]{2,1,0:T(8,128)(2,1)S(1)}, u32[]{:S(2)}, u32[]{:S(2)}) %collective-permute-start.83) | collective-permute-done | bytes 3261472 | tf_op jit(solution)/shard_map/ppermute | solution.py:31
  1092.7 33.4 %collective-permute-done.85 = bf16[9,56,1120]{2,1,0:T(8,128)(2,1)S(1)} collective-permute-done((bf16[9,56,1120]{2,1,0:T(8,128)(2,1)S(1)}, bf16[9,56,1120]{2,1,0:T(8,128)(2,1)S(1)}, u32[]{:S(2)}, u32[]{:S(2)}) %collective-permute-start.85) | collective-permute-done | bytes 1128992 | tf_op jit(solution)/shard_map/ppermute | solution.py:42
  1241.1 16.6 %collective-permute-done.73 = bf16[512,1120]{0,1:T(8,128)(2,1)} collective-permute-done((bf16[512,1120]{0,1:T(8,128)(2,1)}, bf16[512,1120]{0,1:T(8,128)(2,1)}, u32[]{:S(2)}, u32[]{:S(2)}) %collective-permute-start.73) | collective-permute-done | bytes 1146912 | tf_op jit(solution)/shard_map/ppermute | solution.py:52
  1315.7 10.5 collective-permute-done.96
  1346.0 18.3 %while.308 = (s32[]{:T(128)}, f32[42,56,1120]{2,1,0:T(8,128)}, s32[]{:T(128)}, pred[188]{0:T(512)(128)(4,1)S(1)}, s32[188]{0:T(256)S(1)}, /*index=5*/s32[188]{0:...) while((s32[]{:T(128)}, f32[42,56,1120]{2,1,0:T(8,128)}, ...), condition=%wide.region_104.105_spmd, body=%wide.region_97.104_spmd.sunk | while | flops 28827246592 | bytes 133028312 | solution.py:439
  1364.4 30.2 %shard_map.169 = (f32[42,56,1120]{2,1,0:T(8,128)}, f32[8,1120]{1,0:T(8,128)}) custom-call(s32[42]{0:T(128)} %get-tuple-element.4078.kind_ref, s32[42]{0:T(128)} %get-tuple-element.4080.e_at, s32[42]{0:T(128)} %get-tuple-element.4079.f_at, s32[42]{0:T(128)} %get-tuple-element.4077.a_at, f32[42,56,1120]{2,1,0:T(8,128)} %get-tuple-element.3237.rows_ref, ...), custom_call_target="tpu_custom_call" | custom-call | tf_op jit(solution)/shard_map/pallas_call | solution.py:411
  1427.8 27.2 %multiply_subtract_fusion = (f32[42,56,1120]{2,1,0:T(8,128)}, f32[42,56,1120]{2,1,0:T(8,128)}, f32[42,56,1120]{2,1,0:T(8,128)}) fusion(f32[42,56,1120]{2,1,0:T(8,128)} %param.52, f32[42,56,1120]{2,1,0:T(8,128)} %get-tuple-element.3245, f32[]{:T(128)S(6)} %min.858, f32[42,56,1120]{2,1,0:T(8,128)} %param.53, f32[42,56,1120]{2,1,0:T(8,128)} %param.54), kind=kLoop, calls=%fused_computation.173 | loop fusion | flops 42147840 | bytes 73758720 | tf_op jit(solution)/shard_map/sub | solution.py:446
  (963 shorter events, 858.4 us)
Async XLA Ops:
  37.2 208.8 %collective-permute-start.54 = (bf16[21,56,1120]{2,1,0:T(8,128)(2,1)}, bf16[21,56,1120]{2,1,0:T(8,128)(2,1)}, u32[]{:S(2)}, u32[]{:S(2)}) collective-permute-start(bf16[21,56,1120]{2,1,0:T(8,128)(2,1)} %constant_dynamic-slice_fusion.26), channel_id=1, source_target_pairs={{0,8},{2,10},{4,12},{6,14},{8,16},{9,1},{10,18},{11,3},{12,20},{13... | collective-permute-start | bytes 7902728 | tf_op jit(solution)/shard_map/ppermute | solution.py:42
  43.7 59.4 %collective-permute-start.26 = (s32[1,2,1028]{2,1,0:T(2,128)S(1)}, s32[1,2,1028]{2,1,0:T(2,128)S(1)}, u32[]{:S(2)}, u32[]{:S(2)}) collective-permute-start(s32[1,2,1028]{2,1,0:T(2,128)S(1)} %bitcast.403), channel_id=1, source_target_pairs={{0,4},{4,0},{8,12},{12,8},{16,20},{20,16},{24,28},{28,24},{1,5},{5... | collective-permute-start | bytes 24680 | tf_op jit(solution)/shard_map/ppermute | solution.py:47
  63.2 68.8 %collective-permute-start.32 = (bf16[5,56,1120]{2,1,0:T(8,128)(2,1)}, bf16[5,56,1120]{2,1,0:T(8,128)(2,1)}, u32[]{:S(2)}, u32[]{:S(2)}) collective-permute-start(bf16[5,56,1120]{2,1,0:T(8,128)(2,1)} %constant_dynamic-slice_fusion.47), channel_id=1, source_target_pairs={{0,8},{2,10},{4,12},{6,14},{8,16},{9,1},{10,18},{11,3},{12,20},{13... | collective-permute-start | bytes 1881608 | tf_op jit(solution)/shard_map/ppermute | solution.py:42
  85.7 74.1 %collective-permute-start.42 = (bf16[9,56,1120]{2,1,0:T(8,128)(2,1)}, bf16[9,56,1120]{2,1,0:T(8,128)(2,1)}, u32[]{:S(2)}, u32[]{:S(2)}) collective-permute-start(bf16[9,56,1120]{2,1,0:T(8,128)(2,1)} %constant_dynamic-slice_fusion.36), channel_id=1, source_target_pairs={{0,8},{2,10},{4,12},{6,14},{8,16},{9,1},{10,18},{11,3},{12,20},{13... | collective-permute-start | bytes 3386888 | tf_op jit(solution)/shard_map/ppermute | solution.py:42
  252.7 65.1 %collective-permute-start.55 = (bf16[21,56,1120]{2,1,0:T(8,128)(2,1)}, bf16[21,56,1120]{2,1,0:T(8,128)(2,1)}, u32[]{:S(2)}, u32[]{:S(2)}) collective-permute-start(bf16[21,56,1120]{2,1,0:T(8,128)(2,1)} %get-tuple-element.3959), channel_id=1, source_target_pairs={{1,9},{3,11},{5,13},{7,15},{8,0},{9,17},{10,2},{11,19},{12,4},{13,... | collective-permute-start | bytes 7902728 | tf_op jit(solution)/shard_map/ppermute | solution.py:42
  342.0 65.6 %collective-permute-start.48 = (bf16[26,56,1120]{2,1,0:T(8,128)(2,1)}, bf16[26,56,1120]{2,1,0:T(8,128)(2,1)}, u32[]{:S(2)}, u32[]{:S(2)}) collective-permute-start(bf16[26,56,1120]{2,1,0:T(8,128)(2,1)} %constant_dynamic-slice_fusion.29), channel_id=1, source_target_pairs={{0,4},{4,0},{8,12},{12,8},{16,20},{20,16},{24,28},{28,24},{1,5},{5... | collective-permute-start | bytes 9784328 | tf_op jit(solution)/shard_map/ppermute | solution.py:31
  366.3 74.8 %collective-permute-start.57 = (bf16[21,56,1120]{2,1,0:T(8,128)(2,1)}, bf16[21,56,1120]{2,1,0:T(8,128)(2,1)}, u32[]{:S(2)}, u32[]{:S(2)}) collective-permute-start(bf16[21,56,1120]{2,1,0:T(8,128)(2,1)} %get-tuple-element.3955), channel_id=1, source_target_pairs={{1,9},{3,11},{5,13},{7,15},{8,0},{9,17},{10,2},{11,19},{12,4},{13,... | collective-permute-start | bytes 7902728 | tf_op jit(solution)/shard_map/ppermute | solution.py:42
  370.1 53.4 %collective-permute-start.41 = (f32[512,1120]{0,1:T(8,128)}, f32[512,1120]{0,1:T(8,128)}, u32[]{:S(2)}, u32[]{:S(2)}) collective-permute-start(f32[512,1120]{0,1:T(8,128)} %convert_add_fusion.4), channel_id=1, source_target_pairs={{0,1},{1,0},{2,3},{3,2},{4,5},{5,4},{6,7},{7,6},{8,9},{9,8},{10,11... | collective-permute-start | bytes 6881288 | tf_op jit(solution)/shard_map/ppermute | solution.py:52
  751.3 55.4 %collective-permute-start.65 = (f32[2,512,1120]{1,2,0:T(8,128)S(1)}, f32[2,512,1120]{1,2,0:T(8,128)}, u32[]{:S(2)}, u32[]{:S(2)}) collective-permute-start(f32[2,512,1120]{1,2,0:T(8,128)S(1)} %constant_dynamic-slice_fusion.17), channel_id=1, source_target_pairs={{0,1},{1,0},{2,3},{3,2},{4,5},{5,4},{6,7},{7,6},{8,9},{9,8},{10,11... | collective-permute-start | bytes 13762568 | tf_op jit(solution)/shard_map/ppermute | solution.py:52
  799.3 60.6 %collective-permute-start.75 = (bf16[21,56,1120]{2,1,0:T(8,128)(2,1)}, bf16[21,56,1120]{2,1,0:T(8,128)(2,1)}, u32[]{:S(2)}, u32[]{:S(2)}) collective-permute-start(bf16[21,56,1120]{2,1,0:T(8,128)(2,1)} %get-tuple-element.3946), channel_id=1, source_target_pairs={{1,9},{3,11},{5,13},{7,15},{8,0},{9,17},{10,2},{11,19},{12,4},{13,... | collective-permute-start | bytes 7902728 | tf_op jit(solution)/shard_map/ppermute | solution.py:42
  800.6 78.3 %collective-permute-start.76 = (bf16[21,56,1120]{2,1,0:T(8,128)(2,1)}, bf16[21,56,1120]{2,1,0:T(8,128)(2,1)}, u32[]{:S(2)}, u32[]{:S(2)}) collective-permute-start(bf16[21,56,1120]{2,1,0:T(8,128)(2,1)} %get-tuple-element.3945), channel_id=1, source_target_pairs={{0,8},{2,10},{4,12},{6,14},{8,16},{9,1},{10,18},{11,3},{12,20},{13... | collective-permute-start | bytes 7902728 | tf_op jit(solution)/shard_map/ppermute | solution.py:42
  877.2 53.6 %collective-permute-start.68 = (f32[512,1120]{0,1:T(8,128)S(1)}, f32[512,1120]{0,1:T(8,128)S(1)}, u32[]{:S(2)}, u32[]{:S(2)}) collective-permute-start(f32[512,1120]{0,1:T(8,128)S(1)} %convert_add_fusion.2), channel_id=1, source_target_pairs={{0,1},{1,0},{2,3},{3,2},{4,5},{5,4},{6,7},{7,6},{8,9},{9,8},{10,11... | collective-permute-start | bytes 6881288 | tf_op jit(solution)/shard_map/ppermute | solution.py:52
  889.5 91.0 %collective-permute-start.78 = (bf16[21,56,1120]{2,1,0:T(8,128)(2,1)}, bf16[21,56,1120]{2,1,0:T(8,128)(2,1)S(1)}, u32[]{:S(2)}, u32[]{:S(2)}) collective-permute-start(bf16[21,56,1120]{2,1,0:T(8,128)(2,1)} %dynamic-slice_convert_fusion.15), channel_id=1, source_target_pairs={{0,8},{2,10},{4,12},{6,14},{8,16},{9,1},{10,18},{11,3},{12,20},{13... | collective-permute-start | bytes 7902728 | tf_op jit(solution)/shard_map/ppermute | solution.py:42
  929.2 70.3 %collective-permute-start.79 = (bf16[21,56,1120]{2,1,0:T(8,128)(2,1)}, bf16[21,56,1120]{2,1,0:T(8,128)(2,1)}, u32[]{:S(2)}, u32[]{:S(2)}) collective-permute-start(bf16[21,56,1120]{2,1,0:T(8,128)(2,1)} %dynamic-slice_convert_fusion.14), channel_id=1, source_target_pairs={{1,9},{3,11},{5,13},{7,15},{8,0},{9,17},{10,2},{11,19},{12,4},{13,... | collective-permute-start | bytes 7902728 | tf_op jit(solution)/shard_map/ppermute | solution.py:42
  975.9 68.7 %collective-permute-start.83 = (bf16[26,56,1120]{2,1,0:T(8,128)(2,1)S(1)}, bf16[26,56,1120]{2,1,0:T(8,128)(2,1)S(1)}, u32[]{:S(2)}, u32[]{:S(2)}) collective-permute-start(bf16[26,56,1120]{2,1,0:T(8,128)(2,1)S(1)} %dynamic-slice_convert_fusion.10), channel_id=1, source_target_pairs={{0,4},{4,0},{8,12},{12,8},{16,20},{20,16},{24,28},{28,24},{1,5},{5... | collective-permute-start | bytes 9784328 | tf_op jit(solution)/shard_map/ppermute | solution.py:31
  991.6 63.8 %collective-permute-start.80 = (bf16[21,56,1120]{2,1,0:T(8,128)(2,1)}, bf16[21,56,1120]{2,1,0:T(8,128)(2,1)}, u32[]{:S(2)}, u32[]{:S(2)}) collective-permute-start(bf16[21,56,1120]{2,1,0:T(8,128)(2,1)} %dynamic-slice_convert_fusion.13), channel_id=1, source_target_pairs={{0,8},{2,10},{4,12},{6,14},{8,16},{9,1},{10,18},{11,3},{12,20},{13... | collective-permute-start | bytes 7902728 | tf_op jit(solution)/shard_map/ppermute | solution.py:42
  1010.1 76.0 %collective-permute-start.81 = (bf16[21,56,1120]{2,1,0:T(8,128)(2,1)}, bf16[21,56,1120]{2,1,0:T(8,128)(2,1)}, u32[]{:S(2)}, u32[]{:S(2)}) collective-permute-start(bf16[21,56,1120]{2,1,0:T(8,128)(2,1)} %dynamic-slice_convert_fusion.12), channel_id=1, source_target_pairs={{1,9},{3,11},{5,13},{7,15},{8,0},{9,17},{10,2},{11,19},{12,4},{13,... | collective-permute-start | bytes 7902728 | tf_op jit(solution)/shard_map/ppermute | solution.py:42
  1013.2 61.8 %collective-permute-start.70 = (bf16[512,1120]{0,1:T(8,128)(2,1)}, bf16[512,1120]{0,1:T(8,128)(2,1)}, u32[]{:S(2)}, u32[]{:S(2)}) collective-permute-start(bf16[512,1120]{0,1:T(8,128)(2,1)} %fusion.82), channel_id=1, source_target_pairs={{0,2},{1,3},{2,0},{3,1},{4,6},{5,7},{6,4},{7,5},{8,10},{9,11},{10,... | collective-permute-start | bytes 3440648 | tf_op jit(solution)/shard_map/ppermute | solution.py:52
  1066.4 127.2 %collective-permute-start.82 = (bf16[21,56,1120]{2,1,0:T(8,128)(2,1)}, bf16[21,56,1120]{2,1,0:T(8,128)(2,1)}, u32[]{:S(2)}, u32[]{:S(2)}) collective-permute-start(bf16[21,56,1120]{2,1,0:T(8,128)(2,1)} %dynamic-slice_convert_fusion.11), channel_id=1, source_target_pairs={{0,8},{2,10},{4,12},{6,14},{8,16},{9,1},{10,18},{11,3},{12,20},{13... | collective-permute-start | bytes 7902728 | tf_op jit(solution)/shard_map/ppermute | solution.py:42
  1077.0 68.4 %collective-permute-start.71 = (f32[512,1120]{0,1:T(8,128)S(1)}, f32[512,1120]{0,1:T(8,128)S(1)}, u32[]{:S(2)}, u32[]{:S(2)}) collective-permute-start(f32[512,1120]{0,1:T(8,128)S(1)} %convert_add_fusion.1), channel_id=1, source_target_pairs={{0,1},{1,0},{2,3},{3,2},{4,5},{5,4},{6,7},{7,6},{8,9},{9,8},{10,11... | collective-permute-start | bytes 6881288 | tf_op jit(solution)/shard_map/ppermute | solution.py:52
  1084.7 53.0 %collective-permute-start.86 = (bf16[9,56,1120]{2,1,0:T(8,128)(2,1)S(1)}, bf16[9,56,1120]{2,1,0:T(8,128)(2,1)S(1)}, u32[]{:S(2)}, u32[]{:S(2)}) collective-permute-start(bf16[9,56,1120]{2,1,0:T(8,128)(2,1)S(1)} %dynamic-slice_convert_fusion.23), channel_id=1, source_target_pairs={{1,9},{3,11},{5,13},{7,15},{8,0},{9,17},{10,2},{11,19},{12,4},{13,... | collective-permute-start | bytes 3386888 | tf_op jit(solution)/shard_map/ppermute | solution.py:42
  1132.3 69.2 %collective-permute-start.87 = (bf16[9,56,1120]{2,1,0:T(8,128)(2,1)}, bf16[9,56,1120]{2,1,0:T(8,128)(2,1)}, u32[]{:S(2)}, u32[]{:S(2)}) collective-permute-start(bf16[9,56,1120]{2,1,0:T(8,128)(2,1)} %dynamic-slice_convert_fusion.22), channel_id=1, source_target_pairs={{0,8},{2,10},{4,12},{6,14},{8,16},{9,1},{10,18},{11,3},{12,20},{13... | collective-permute-start | bytes 3386888 | tf_op jit(solution)/shard_map/ppermute | solution.py:42
  1144.0 70.9 %collective-permute-start.88 = (bf16[9,56,1120]{2,1,0:T(8,128)(2,1)}, bf16[9,56,1120]{2,1,0:T(8,128)(2,1)}, u32[]{:S(2)}, u32[]{:S(2)}) collective-permute-start(bf16[9,56,1120]{2,1,0:T(8,128)(2,1)} %dynamic-slice_convert_fusion.21), channel_id=1, source_target_pairs={{1,9},{3,11},{5,13},{7,15},{8,0},{9,17},{10,2},{11,19},{12,4},{13,... | collective-permute-start | bytes 3386888 | tf_op jit(solution)/shard_map/ppermute | solution.py:42
  1207.9 101.4 %collective-permute-start.89 = (bf16[9,56,1120]{2,1,0:T(8,128)(2,1)}, bf16[9,56,1120]{2,1,0:T(8,128)(2,1)}, u32[]{:S(2)}, u32[]{:S(2)}) collective-permute-start(bf16[9,56,1120]{2,1,0:T(8,128)(2,1)} %dynamic-slice_convert_fusion.20), channel_id=1, source_target_pairs={{0,8},{2,10},{4,12},{6,14},{8,16},{9,1},{10,18},{11,3},{12,20},{13... | collective-permute-start | bytes 3386888 | tf_op jit(solution)/shard_map/ppermute | solution.py:42
  (268 other events, 4584.3 us)

commit v2 on v1

--- a/solution.py
+++ b/solution.py
@@ -2,6 +2,8 @@
 import jax.numpy as jnp
 from jax import lax
 from jax.experimental import pallas as pl
+from jax.experimental.layout import Layout as Order
+from jax.experimental.layout import with_layout_constraint
 from jax.experimental.pallas import tpu as pltpu
 from jax.sharding import PartitionSpec as P
 
@@ -192,7 +194,8 @@
     place = lax.broadcasted_iota(jnp.int32, block.shape, 0)
     good = (place >= least) & (place < limit)
     if add:
-        new = old + jnp.where(good, block.astype(old.dtype), 0)
+        new = old.astype(F32) + jnp.where(good, block.astype(F32), 0.0)
+        new = new.astype(old.dtype)
     else:
         new = jnp.where(good, block, old)
     return lax.dynamic_update_slice_in_dim(store, new, start, 0)
@@ -388,7 +391,7 @@
 def assemble_kernel(kind_ref, e_at, f_at, a_at, rows_ref, e_ref, f_ref, a_ref, out_ref, sq_ref):
     slot = pl.program_id(0)
     kind = kind_ref[slot]
-    value = jnp.where(kind == 0, e_ref[...], 0.0)
+    value = jnp.where(kind == 0, e_ref[...].astype(F32), 0.0)
     value = jnp.where(kind == 1, f_ref[...], value)
     value = rows_ref[...] + jnp.where(kind == 2, a_ref[...], value)
     out_ref[...] = value
@@ -406,7 +409,15 @@
     kind = jnp.full((slots,), 3, jnp.int32)
     for number, at in enumerate(index):
         kind = jnp.where(at >= 0, number, kind)
-    index = [jnp.maximum(at, 0).astype(jnp.int32) for at in index]
+    places = jnp.arange(slots)
+
+    def held(at):
+        used = jnp.where((at >= 0)[None, :] & (places[None, :] <= places[:, None]), places, -1)
+        latest = jnp.max(used, axis=1)
+        same = places[None, :] == latest[:, None]
+        return jnp.sum(jnp.where(same, at[None, :], 0), axis=1).astype(jnp.int32)
+
+    index = [held(at) for at in index]
     block = (1, rows_unit, width)
     return pl.pallas_call(
         assemble_kernel,
@@ -664,7 +675,8 @@
     part, sent = halved(dot_plain(d_logits, table))
     d_logits, sent = together(d_logits, sent)
     swapped = mp_flip(sent, 1)
-    grad_e = dot_first(d_logits, both).reshape(usual, rows_unit, width)
+    grad_e = with_layout_constraint(dot_first(d_logits, both), Order((0, 1))).astype(BF16)
+    grad_e = grad_e.reshape(usual, rows_unit, width)
     part = part + swapped
     collect_e = Collect(grad_e, lay_m, 21, 4)
     collect_e.launch()
@@ -743,23 +755,34 @@
     def take(turn, rows):
         return dot_first(owner_picks(turn), rows.reshape(dp * PICK, width))
 
-    rows = collect_a.step(collect_f.step(give(0)))
-    owned = take(0, rows)
-    owned = lax.fori_loop(1, rounds, lambda i, t: t + take(i, give(i)), owned)
+    collect_f.step()
+    collect_a.step()
+    collect_a.step()
+    collect_f.land()
+    collect_a.land()
+
+    def more_owned(owned, own, both, lse):
+        grad = dot_first(slopes(*scores(spill(own), lay_t, usual, both), lse), both)
+        stream = Collect(grad.reshape(-1, rows_unit, width), lay_t, 8, 0)
+        stream.rest()
+        index = lay_t.at_slot(slots)
+        block = stream.store[jnp.maximum(index, 0)]
+        block = jnp.where((index >= 0)[:, None, None], block, 0.0)
+        return owned + block.reshape(owned.shape)
+
+    def more(i, owned):
+        if lay_t is None:
+            return owned + take(i, give(i))
+        j, *held = together(i, own, both, lse)
+        return lax.cond(
+            j < rounds,
+            lambda: owned + take(j, give(j)),
+            lambda: more_owned(owned, *held),
+        )
+
+    turns = rounds if lay_t is None else rounds + crowded.astype(jnp.int32)
+    owned = lax.fori_loop(1, turns, more, take(0, give(0)))
     owned = owned.reshape(slots, rows_unit, width)
-    owned = collect_a.step(owned)
-    if lay_t is not None:
-
-        def more_owned(owned, own, both, lse):
-            grad = dot_first(slopes(*scores(spill(own), lay_t, usual, both), lse), both)
-            stream = Collect(grad.reshape(-1, rows_unit, width), lay_t, 8, 0)
-            stream.rest()
-            index = lay_t.at_slot(slots)
-            block = stream.store[jnp.maximum(index, 0)]
-            return owned + jnp.where((index >= 0)[:, None, None], block, 0.0)
-
-        owned = when(crowded, more_owned, owned, own, both, lse)
-    owned = collect_a.land(collect_f.land(owned))
     grad_f, grad_a = collect_f.finish(), collect_a.finish()
     index = [lay.at_slot(slots) for lay in (lay_m, lay_f, lay_a)]
     owned, squares = assemble(owned, (grad_e, grad_f, grad_a), index)

time: 1470 us -> 1450 us (0.986)
  other arithmetic: 414 us -> 398 us
    dynamic_update_slice x27 -> x20, other arithmetic: 115 us -> 45.8 us  [put(): return lax.dynamic_update_slice_in_dim(store, new, start, 0)]
    dynamic_slice x17 -> x24, other arithmetic: 74.3 us -> 124 us  [window(): return (start, lax.dynamic_slice_in_dim(store, start, chunk, 0))]
    convert_element_type x17 -> x10, local copies, waits for them, and re-layouts: 55.5 us -> 13.3 us  [outgoing(): return window(store, self.edges(k, lane)[1], self.chunk)[1].astype(BF16)]
    ppermute x7, waiting for transfers between devices: 99.1 us -> 119 us  [dp_pair(): return lax.ppermute(value, 'dp', [(d, d ^ 1) for d in range(size)])]
    unnamed x435 -> x451, local copies, waits for them, and re-layouts: 18.5 us -> 37.6 us
  transfers between devices with their start and end apart: 78 -> 78, of which waited for: 33 -> 36; matrix products, arithmetic and copies ran while one was open for 41% -> 38% of each run, Pallas kernels for 0% -> 0%
where the time goes in v2:
time: 1450 us; the launch traced here: 1440 us
  other arithmetic  398 us (27%)
  waiting for transfers between devices  343 us (24%)
  starting transfers between devices  207 us (14%)
  matrix products  206 us (14%)
  local copies, waits for them, and re-layouts  183 us (13%)
  between operations  58.8 us (4%)
  Pallas kernels  28 us (2%)
    ppermute x40, waiting for transfers between devices, line_hop(): return lax.ppermute(value, ('dp', 'mp'), moves)  186 us
    ppermute x40, starting transfers between devices, line_hop(): return lax.ppermute(value, ('dp', 'mp'), moves)  141 us
    dynamic_slice x24, other arithmetic, window(): return (start, lax.dynamic_slice_in_dim(store, start, chunk, 0))  124 us
    ppermute x7, waiting for transfers between devices, dp_pair(): return lax.ppermute(value, 'dp', [(d, d ^ 1) for d in range(size)])  119 us
    dot_general x7, matrix products, dot_plain(): return jnp.dot(left, right, preferred_element_type=F32)  64.4 us
    dot_general x8, matrix products, dot_first(): lax.dot_general(left, right, (((0,), (0,)), ((), ())), preferred_element_...  64 us
    dot_general x5, matrix products, dot_t(): lax.dot_general(left, right, (((1,), (1,)), ((), ())), preferred_element_...  55.4 us
    dynamic_update_slice x20, other arithmetic, put(): return lax.dynamic_update_slice_in_dim(store, new, start, 0)  45.8 us
  transfers between devices with their start and end apart: 78, of which 36 were waited for; matrix products, arithmetic and copies ran while one was open for 38% of the time, Pallas kernels for 0%

profile of v2, /device:TPU:0, one launch (start us, length us, event | category | flops | bytes accessed | tf_op | source)
XLA Modules:
  0.0 1435.6 jit_solution(6778027850554116654)
XLA Ops:
  23.5 10.0 gather_fusion.8
  120.9 9.8 convert_reduce_fusion
  165.1 18.3 %collective-permute-done.34 = bf16[5,56,1120]{2,1,0:T(8,128)(2,1)} collective-permute-done((bf16[5,56,1120]{2,1,0:T(8,128)(2,1)}, bf16[5,56,1120]{2,1,0:T(8,128)(2,1)}, u32[]{:S(2)}, u32[]{:S(2)}) %collective-permute-start.34) | collective-permute-done | bytes 627232 | tf_op jit(solution)/shard_map/ppermute | solution.py:44
  226.3 12.9 collective-permute-done.44
  376.6 31.5 %collective-permute-done.48 = bf16[26,56,1120]{2,1,0:T(8,128)(2,1)} collective-permute-done((bf16[26,56,1120]{2,1,0:T(8,128)(2,1)}, bf16[26,56,1120]{2,1,0:T(8,128)(2,1)}, u32[]{:S(2)}, u32[]{:S(2)}) %collective-permute-start.48) | collective-permute-done | bytes 3261472 | tf_op jit(solution)/shard_map/ppermute | solution.py:33
  461.1 23.5 %collective-permute-done.58 = bf16[21,56,1120]{2,1,0:T(8,128)(2,1)} collective-permute-done((bf16[21,56,1120]{2,1,0:T(8,128)(2,1)}, bf16[21,56,1120]{2,1,0:T(8,128)(2,1)}, u32[]{:S(2)}, u32[]{:S(2)}) %collective-permute-start.58) | collective-permute-done | bytes 2634272 | tf_op jit(solution)/shard_map/ppermute | solution.py:44
  544.2 23.0 %collective-permute-done.60 = bf16[21,56,1120]{2,1,0:T(8,128)(2,1)S(1)} collective-permute-done((bf16[21,56,1120]{2,1,0:T(8,128)(2,1)S(1)}, bf16[21,56,1120]{2,1,0:T(8,128)(2,1)S(1)}, u32[]{:S(2)}, u32[]{:S(2)}) %collective-permute-start.60) | collective-permute-done | bytes 2634272 | tf_op jit(solution)/shard_map/ppermute | solution.py:44
  591.5 16.9 %collective-permute-done.61 = bf16[21,56,1120]{2,1,0:T(8,128)(2,1)} collective-permute-done((bf16[21,56,1120]{2,1,0:T(8,128)(2,1)}, bf16[21,56,1120]{2,1,0:T(8,128)(2,1)}, u32[]{:S(2)}, u32[]{:S(2)}) %collective-permute-start.61) | collective-permute-done | bytes 2634272 | tf_op jit(solution)/shard_map/ppermute | solution.py:44
  613.3 41.4 %select_reduce_fusion.11 = (f32[2048]{0:T(1024)S(1)}, f32[2048,6272]{1,0:T(8,128)}) fusion(pred[6272]{0:T(1024)(128)(4,1)S(1)} %iota_compare_fusion.36, bf16[6272,1120]{1,0:T(8,128)(2,1)} %bitcast.66, bf16[512,1120]{0,1:T(8,128)(2,1)S(1)} %copy-done.44, bf16[512,1120]{0,1:T(8,128)(2,1)S(1)} %get-tuple-element.3421, ...), kind=kOutput, calls=%fused_computation.197 | convolution fusion | flops 28812376064 | bytes 70031488 | tf_op jit(solution)/shard_map/dot_general | solution.py:370
  654.7 18.1 %select_reduce_fusion.10 = (f32[2048]{0:T(1024)S(1)}, f32[2048]{0:T(1024)S(1)}) fusion(f32[2048,6272]{1,0:T(8,128)} %get-tuple-element.3506, f32[2048]{0:T(1024)S(1)} %get-tuple-element.3505, pred[6272]{0:T(1024)(128)(4,1)S(1)} %iota_compare_fusion.36, s32[2048]{0:T(1024)S(1)} %fusion.132), kind=kLoop, calls=%fused_computation.196 | loop fusion | flops 77066240 | bytes 51419264 | tf_op jit(solution)/shard_map/reduce_sum | solution.py:638
  684.0 26.6 %multiply_convert_fusion.1 = bf16[2048,6272]{1,0:T(8,128)(2,1)} fusion(f32[2048,6272]{1,0:T(8,128)} %get-tuple-element.3506, f32[2048]{0:T(1024)} %log_add_fusion, s32[2048]{0:T(1024)S(1)} %get-tuple-element.5688, f32[2048]{0:T(1024)S(1)} %bitcast.403, pred[6272]{0:T(1024)(128)(4,1)S(1)} %copy-done.113), kind=kLoop, calls=%fused_computation.193 | loop fusion | flops 89915392 | bytes 77101184 | tf_op jit(solution)/shard_map/convert_element_type | solution.py:644
  710.7 41.1 %fusion.198 = f32[2,1024,1120]{1,2,0:T(8,128)S(1)} fusion(bf16[2,1024,6272]{2,1,0:T(8,128)(2,1)} %bitcast.364, bf16[6272,1120,1]{1,0,2:T(8,128)(2,1)} %bitcast.82), kind=kOutput, calls=%fused_computation.840 | convolution fusion | flops 28772925440 | bytes 48914432 | tf_op jit(solution)/shard_map/dot_general | solution.py:378
  757.9 37.0 %convolution_convert_fusion.1 = bf16[6272,1120]{1,0:T(8,128)(2,1)S(1)} fusion(bf16[2048,6272]{1,0:T(8,128)(2,1)} %multiply_convert_fusion.1, bf16[512,1120]{0,1:T(8,128)(2,1)S(1)} %copy-done.45, bf16[512,1120]{0,1:T(8,128)(2,1)S(1)} %copy-done.42, bf16[1024,1120]{0,1:T(8,128)(2,1)S(1)} %copy-done.26), kind=kOutput, calls=%fused_computation.200 | convolution fusion | flops 28793712640 | bytes 44326912 | tf_op jit(solution)/shard_map/dot_general | solution.py:374
  817.4 18.6 %collective-permute-done.66 = bf16[512,1120]{0,1:T(8,128)(2,1)} collective-permute-done((bf16[512,1120]{0,1:T(8,128)(2,1)}, bf16[512,1120]{0,1:T(8,128)(2,1)}, u32[]{:S(2)}, u32[]{:S(2)}) %collective-permute-start.66) | collective-permute-done | bytes 1146912 | tf_op jit(solution)/shard_map/ppermute | solution.py:33
  871.5 13.8 collective-permute-done.76
  925.4 11.5 gather_fusion.9
  972.1 42.3 %collective-permute-done.83 = bf16[26,56,1120]{2,1,0:T(8,128)(2,1)} collective-permute-done((bf16[26,56,1120]{2,1,0:T(8,128)(2,1)}, bf16[26,56,1120]{2,1,0:T(8,128)(2,1)}, u32[]{:S(2)}, u32[]{:S(2)}) %collective-permute-start.83) | collective-permute-done | bytes 3261472 | tf_op jit(solution)/shard_map/ppermute | solution.py:33
  1038.4 10.0 collective-permute-start.85
  1059.0 15.3 %collective-permute-done.85 = bf16[9,56,1120]{2,1,0:T(8,128)(2,1)S(1)} collective-permute-done((bf16[9,56,1120]{2,1,0:T(8,128)(2,1)S(1)}, bf16[9,56,1120]{2,1,0:T(8,128)(2,1)S(1)}, u32[]{:S(2)}, u32[]{:S(2)}) %collective-permute-start.85) | collective-permute-done | bytes 1128992 | tf_op jit(solution)/shard_map/ppermute | solution.py:44
  1107.9 9.3 collective-permute-done.86
  1192.0 18.8 %collective-permute-done.90 = bf16[13,56,1120]{2,1,0:T(8,128)(2,1)S(1)} collective-permute-done((bf16[13,56,1120]{2,1,0:T(8,128)(2,1)S(1)}, bf16[13,56,1120]{2,1,0:T(8,128)(2,1)S(1)}, u32[]{:S(2)}, u32[]{:S(2)}) %collective-permute-start.90) | collective-permute-done | bytes 1630752 | tf_op jit(solution)/shard_map/ppermute | solution.py:33
  1229.3 9.9 collective-permute-done.91
  1345.3 28.0 %shard_map.169 = (f32[42,56,1120]{2,1,0:T(8,128)}, f32[8,1120]{1,0:T(8,128)}) custom-call(s32[42]{0:T(128)} %get-tuple-element.3500.kind_ref, s32[42]{0:T(128)} %select_reduce_fusion.23.e_at, s32[42]{0:T(128)} %get-tuple-element.3511.f_at, s32[42]{0:T(128)} %get-tuple-element.3510.a_at, f32[42,56,1120]{2,1,0:T(8,128)} %bitcast.338, ...), custom_call_target="tpu_custom_call" | custom-call | tf_op jit(solution)/shard_map/pallas_call | solution.py:422
  1407.1 27.2 %multiply_subtract_fusion = (f32[42,56,1120]{2,1,0:T(8,128)}, f32[42,56,1120]{2,1,0:T(8,128)}, f32[42,56,1120]{2,1,0:T(8,128)}) fusion(f32[42,56,1120]{2,1,0:T(8,128)} %param.52, f32[42,56,1120]{2,1,0:T(8,128)} %get-tuple-element.2720, f32[]{:T(128)S(6)} %min.858, f32[42,56,1120]{2,1,0:T(8,128)} %param.53, f32[42,56,1120]{2,1,0:T(8,128)} %param.54), kind=kLoop, calls=%fused_computation.203 | loop fusion | flops 42147840 | bytes 73758720 | tf_op jit(solution)/shard_map/sub | solution.py:457
  (984 shorter events, 862.5 us)
Async XLA Ops:
  37.0 209.1 %collective-permute-start.54 = (bf16[21,56,1120]{2,1,0:T(8,128)(2,1)}, bf16[21,56,1120]{2,1,0:T(8,128)(2,1)}, u32[]{:S(2)}, u32[]{:S(2)}) collective-permute-start(bf16[21,56,1120]{2,1,0:T(8,128)(2,1)} %constant_dynamic-slice_fusion.36), channel_id=1, source_target_pairs={{0,8},{2,10},{4,12},{6,14},{8,16},{9,1},{10,18},{11,3},{12,20},{13... | collective-permute-start | bytes 7902728 | tf_op jit(solution)/shard_map/ppermute | solution.py:44
  43.7 59.5 %collective-permute-start.26 = (s32[1,2,1028]{2,1,0:T(2,128)S(1)}, s32[1,2,1028]{2,1,0:T(2,128)S(1)}, u32[]{:S(2)}, u32[]{:S(2)}) collective-permute-start(s32[1,2,1028]{2,1,0:T(2,128)S(1)} %bitcast.406), channel_id=1, source_target_pairs={{0,4},{4,0},{8,12},{12,8},{16,20},{20,16},{24,28},{28,24},{1,5},{5... | collective-permute-start | bytes 24680 | tf_op jit(solution)/shard_map/ppermute | solution.py:49
  63.0 69.0 %collective-permute-start.32 = (bf16[5,56,1120]{2,1,0:T(8,128)(2,1)}, bf16[5,56,1120]{2,1,0:T(8,128)(2,1)}, u32[]{:S(2)}, u32[]{:S(2)}) collective-permute-start(bf16[5,56,1120]{2,1,0:T(8,128)(2,1)} %constant_dynamic-slice_fusion.57), channel_id=1, source_target_pairs={{0,8},{2,10},{4,12},{6,14},{8,16},{9,1},{10,18},{11,3},{12,20},{13... | collective-permute-start | bytes 1881608 | tf_op jit(solution)/shard_map/ppermute | solution.py:44
  86.0 74.0 %collective-permute-start.42 = (bf16[9,56,1120]{2,1,0:T(8,128)(2,1)}, bf16[9,56,1120]{2,1,0:T(8,128)(2,1)}, u32[]{:S(2)}, u32[]{:S(2)}) collective-permute-start(bf16[9,56,1120]{2,1,0:T(8,128)(2,1)} %constant_dynamic-slice_fusion.46), channel_id=1, source_target_pairs={{0,8},{2,10},{4,12},{6,14},{8,16},{9,1},{10,18},{11,3},{12,20},{13... | collective-permute-start | bytes 3386888 | tf_op jit(solution)/shard_map/ppermute | solution.py:44
  163.8 45.8 %collective-permute-start.43 = (bf16[9,56,1120]{2,1,0:T(8,128)(2,1)}, bf16[9,56,1120]{2,1,0:T(8,128)(2,1)}, u32[]{:S(2)}, u32[]{:S(2)}) collective-permute-start(bf16[9,56,1120]{2,1,0:T(8,128)(2,1)} %get-tuple-element.3399), channel_id=1, source_target_pairs={{1,9},{3,11},{5,13},{7,15},{8,0},{9,17},{10,2},{11,19},{12,4},{13,... | collective-permute-start | bytes 3386888 | tf_op jit(solution)/shard_map/ppermute | solution.py:44
  252.8 65.4 %collective-permute-start.55 = (bf16[21,56,1120]{2,1,0:T(8,128)(2,1)}, bf16[21,56,1120]{2,1,0:T(8,128)(2,1)}, u32[]{:S(2)}, u32[]{:S(2)}) collective-permute-start(bf16[21,56,1120]{2,1,0:T(8,128)(2,1)} %get-tuple-element.3381), channel_id=1, source_target_pairs={{1,9},{3,11},{5,13},{7,15},{8,0},{9,17},{10,2},{11,19},{12,4},{13,... | collective-permute-start | bytes 7902728 | tf_op jit(solution)/shard_map/ppermute | solution.py:44
  264.4 45.9 %collective-permute-start.46 = (bf16[9,56,1120]{2,1,0:T(8,128)(2,1)}, bf16[9,56,1120]{2,1,0:T(8,128)(2,1)}, u32[]{:S(2)}, u32[]{:S(2)}) collective-permute-start(bf16[9,56,1120]{2,1,0:T(8,128)(2,1)} %get-tuple-element.3393), channel_id=1, source_target_pairs={{0,8},{2,10},{4,12},{6,14},{8,16},{9,1},{10,18},{11,3},{12,20},{13... | collective-permute-start | bytes 3386888 | tf_op jit(solution)/shard_map/ppermute | solution.py:44
  342.4 65.7 %collective-permute-start.48 = (bf16[26,56,1120]{2,1,0:T(8,128)(2,1)}, bf16[26,56,1120]{2,1,0:T(8,128)(2,1)}, u32[]{:S(2)}, u32[]{:S(2)}) collective-permute-start(bf16[26,56,1120]{2,1,0:T(8,128)(2,1)} %constant_dynamic-slice_fusion.39), channel_id=1, source_target_pairs={{0,4},{4,0},{8,12},{12,8},{16,20},{20,16},{24,28},{28,24},{1,5},{5... | collective-permute-start | bytes 9784328 | tf_op jit(solution)/shard_map/ppermute | solution.py:33
  366.6 75.4 %collective-permute-start.57 = (bf16[21,56,1120]{2,1,0:T(8,128)(2,1)}, bf16[21,56,1120]{2,1,0:T(8,128)(2,1)}, u32[]{:S(2)}, u32[]{:S(2)}) collective-permute-start(bf16[21,56,1120]{2,1,0:T(8,128)(2,1)} %get-tuple-element.3377), channel_id=1, source_target_pairs={{1,9},{3,11},{5,13},{7,15},{8,0},{9,17},{10,2},{11,19},{12,4},{13,... | collective-permute-start | bytes 7902728 | tf_op jit(solution)/shard_map/ppermute | solution.py:44
  370.0 54.4 %collective-permute-start.41 = (f32[512,1120]{0,1:T(8,128)}, f32[512,1120]{0,1:T(8,128)}, u32[]{:S(2)}, u32[]{:S(2)}) collective-permute-start(f32[512,1120]{0,1:T(8,128)} %convert_add_fusion.4), channel_id=1, source_target_pairs={{0,1},{1,0},{2,3},{3,2},{4,5},{5,4},{6,7},{7,6},{8,9},{9,8},{10,11... | collective-permute-start | bytes 6881288 | tf_op jit(solution)/shard_map/ppermute | solution.py:54
  757.9 45.2 %collective-permute-start.65 = (f32[2,512,1120]{1,2,0:T(8,128)}, f32[2,512,1120]{1,2,0:T(8,128)}, u32[]{:S(2)}, u32[]{:S(2)}) collective-permute-start(f32[2,512,1120]{1,2,0:T(8,128)} %constant_dynamic-slice_fusion.27), channel_id=1, source_target_pairs={{0,1},{1,0},{2,3},{3,2},{4,5},{5,4},{6,7},{7,6},{8,9},{9,8},{10,11... | collective-permute-start | bytes 13762568 | tf_op jit(solution)/shard_map/ppermute | solution.py:54
  891.9 65.0 %collective-permute-start.77 = (bf16[21,56,1120]{2,1,0:T(8,128)(2,1)}, bf16[21,56,1120]{2,1,0:T(8,128)(2,1)}, u32[]{:S(2)}, u32[]{:S(2)}) collective-permute-start(bf16[21,56,1120]{2,1,0:T(8,128)(2,1)} %get-tuple-element.3365), channel_id=1, source_target_pairs={{1,9},{3,11},{5,13},{7,15},{8,0},{9,17},{10,2},{11,19},{12,4},{13,... | collective-permute-start | bytes 7902728 | tf_op jit(solution)/shard_map/ppermute | solution.py:44
  942.1 72.3 %collective-permute-start.83 = (bf16[26,56,1120]{2,1,0:T(8,128)(2,1)}, bf16[26,56,1120]{2,1,0:T(8,128)(2,1)}, u32[]{:S(2)}, u32[]{:S(2)}) collective-permute-start(bf16[26,56,1120]{2,1,0:T(8,128)(2,1)} %dynamic-slice_convert_fusion.8), channel_id=1, source_target_pairs={{0,4},{4,0},{8,12},{12,8},{16,20},{20,16},{24,28},{28,24},{1,5},{5... | collective-permute-start | bytes 9784328 | tf_op jit(solution)/shard_map/ppermute | solution.py:33
  964.2 62.5 %collective-permute-start.78 = (bf16[21,56,1120]{2,1,0:T(8,128)(2,1)}, bf16[21,56,1120]{2,1,0:T(8,128)(2,1)}, u32[]{:S(2)}, u32[]{:S(2)}) collective-permute-start(bf16[21,56,1120]{2,1,0:T(8,128)(2,1)} %get-tuple-element.3363), channel_id=1, source_target_pairs={{0,8},{2,10},{4,12},{6,14},{8,16},{9,1},{10,18},{11,3},{12,20},{13... | collective-permute-start | bytes 7902728 | tf_op jit(solution)/shard_map/ppermute | solution.py:44
  971.5 76.8 %collective-permute-start.70 = (bf16[512,1120]{0,1:T(8,128)(2,1)}, bf16[512,1120]{0,1:T(8,128)(2,1)}, u32[]{:S(2)}, u32[]{:S(2)}) collective-permute-start(bf16[512,1120]{0,1:T(8,128)(2,1)} %fusion.101), channel_id=1, source_target_pairs={{0,2},{1,3},{2,0},{3,1},{4,6},{5,7},{6,4},{7,5},{8,10},{9,11},{10,... | collective-permute-start | bytes 3440648 | tf_op jit(solution)/shard_map/ppermute | solution.py:54
  1033.7 58.6 %collective-permute-start.79 = (bf16[21,56,1120]{2,1,0:T(8,128)(2,1)}, bf16[21,56,1120]{2,1,0:T(8,128)(2,1)}, u32[]{:S(2)}, u32[]{:S(2)}) collective-permute-start(bf16[21,56,1120]{2,1,0:T(8,128)(2,1)} %get-tuple-element.3361), channel_id=1, source_target_pairs={{1,9},{3,11},{5,13},{7,15},{8,0},{9,17},{10,2},{11,19},{12,4},{13,... | collective-permute-start | bytes 7902728 | tf_op jit(solution)/shard_map/ppermute | solution.py:44
  1051.0 79.3 %collective-permute-start.71 = (f32[512,1120]{0,1:T(8,128)S(1)}, f32[512,1120]{0,1:T(8,128)S(1)}, u32[]{:S(2)}, u32[]{:S(2)}) collective-permute-start(f32[512,1120]{0,1:T(8,128)S(1)} %convert_add_fusion.1), channel_id=1, source_target_pairs={{0,1},{1,0},{2,3},{3,2},{4,5},{5,4},{6,7},{7,6},{8,9},{9,8},{10,11... | collective-permute-start | bytes 6881288 | tf_op jit(solution)/shard_map/ppermute | solution.py:54
  1057.5 59.6 %collective-permute-start.86 = (bf16[9,56,1120]{2,1,0:T(8,128)(2,1)S(1)}, bf16[9,56,1120]{2,1,0:T(8,128)(2,1)S(1)}, u32[]{:S(2)}, u32[]{:S(2)}) collective-permute-start(bf16[9,56,1120]{2,1,0:T(8,128)(2,1)S(1)} %dynamic-slice_convert_fusion.13), channel_id=1, source_target_pairs={{1,9},{3,11},{5,13},{7,15},{8,0},{9,17},{10,2},{11,19},{12,4},{13,... | collective-permute-start | bytes 3386888 | tf_op jit(solution)/shard_map/ppermute | solution.py:44
  1099.6 83.4 %collective-permute-start.80 = (bf16[21,56,1120]{2,1,0:T(8,128)(2,1)}, bf16[21,56,1120]{2,1,0:T(8,128)(2,1)}, u32[]{:S(2)}, u32[]{:S(2)}) collective-permute-start(bf16[21,56,1120]{2,1,0:T(8,128)(2,1)} %get-tuple-element.3359), channel_id=1, source_target_pairs={{0,8},{2,10},{4,12},{6,14},{8,16},{9,1},{10,18},{11,3},{12,20},{13... | collective-permute-start | bytes 7902728 | tf_op jit(solution)/shard_map/ppermute | solution.py:44
  1118.8 98.6 %collective-permute-start.88 = (bf16[9,56,1120]{2,1,0:T(8,128)(2,1)}, bf16[9,56,1120]{2,1,0:T(8,128)(2,1)}, u32[]{:S(2)}, u32[]{:S(2)}) collective-permute-start(bf16[9,56,1120]{2,1,0:T(8,128)(2,1)} %dynamic-slice_convert_fusion.11), channel_id=1, source_target_pairs={{1,9},{3,11},{5,13},{7,15},{8,0},{9,17},{10,2},{11,19},{12,4},{13,... | collective-permute-start | bytes 3386888 | tf_op jit(solution)/shard_map/ppermute | solution.py:44
  1121.9 174.3 %collective-permute-start.89 = (bf16[9,56,1120]{2,1,0:T(8,128)(2,1)}, bf16[9,56,1120]{2,1,0:T(8,128)(2,1)}, u32[]{:S(2)}, u32[]{:S(2)}) collective-permute-start(bf16[9,56,1120]{2,1,0:T(8,128)(2,1)} %dynamic-slice_convert_fusion.10), channel_id=1, source_target_pairs={{0,8},{2,10},{4,12},{6,14},{8,16},{9,1},{10,18},{11,3},{12,20},{13... | collective-permute-start | bytes 3386888 | tf_op jit(solution)/shard_map/ppermute | solution.py:44
  1183.1 42.7 %collective-permute-start.72 = (f32[512,1120]{0,1:T(8,128)}, f32[512,1120]{0,1:T(8,128)}, u32[]{:S(2)}, u32[]{:S(2)}) collective-permute-start(f32[512,1120]{0,1:T(8,128)} %constant_dynamic-slice_fusion.25), channel_id=1, source_target_pairs={{0,1},{1,0},{2,3},{3,2},{4,5},{5,4},{6,7},{7,6},{8,9},{9,8},{10,11... | collective-permute-start | bytes 6881288 | tf_op jit(solution)/shard_map/ppermute | solution.py:54
  1190.7 77.7 %collective-permute-start.81 = (bf16[21,56,1120]{2,1,0:T(8,128)(2,1)}, bf16[21,56,1120]{2,1,0:T(8,128)(2,1)}, u32[]{:S(2)}, u32[]{:S(2)}) collective-permute-start(bf16[21,56,1120]{2,1,0:T(8,128)(2,1)} %get-tuple-element.3357), channel_id=1, source_target_pairs={{1,9},{3,11},{5,13},{7,15},{8,0},{9,17},{10,2},{11,19},{12,4},{13,... | collective-permute-start | bytes 7902728 | tf_op jit(solution)/shard_map/ppermute | solution.py:44
  1275.2 42.9 %collective-permute-start.82 = (bf16[21,56,1120]{2,1,0:T(8,128)(2,1)}, bf16[21,56,1120]{2,1,0:T(8,128)(2,1)}, u32[]{:S(2)}, u32[]{:S(2)}) collective-permute-start(bf16[21,56,1120]{2,1,0:T(8,128)(2,1)} %get-tuple-element.3355), channel_id=1, source_target_pairs={{0,8},{2,10},{4,12},{6,14},{8,16},{9,1},{10,18},{11,3},{12,20},{13... | collective-permute-start | bytes 7902728 | tf_op jit(solution)/shard_map/ppermute | solution.py:44
  (276 other events, 5217.1 us)

commit v3 on v2

--- a/solution.py
+++ b/solution.py
@@ -23,7 +23,7 @@
 CLIP_LIMIT = 1.0
 NEG_FILL = -1e30
 
-PICK = 64
+PICK = 48
 F32 = jnp.float32
 BF16 = jnp.bfloat16
 

time: 1450 us -> 1460 us (level)
    ppermute x40, waiting for transfers between devices: 186 us -> 157 us  [line_hop(): return lax.ppermute(value, ('dp', 'mp'), moves)]
    ppermute x7, waiting for transfers between devices: 119 us -> 142 us  [dp_pair(): return lax.ppermute(value, 'dp', [(d, d ^ 1) for d in range(size)])]
    unnamed x451 -> x461, local copies, waits for them, and re-layouts: 37.6 us -> 35.2 us
  transfers between devices with their start and end apart: 78 -> 78, of which waited for: 36 -> 35; matrix products, arithmetic and copies ran while one was open for 38% -> 38% of each run, Pallas kernels for 0% -> 0%
where the time goes in v3:
time: 1460 us; the launch traced here: 1450 us
  other arithmetic  409 us (28%)
  waiting for transfers between devices  337 us (23%)
  starting transfers between devices  218 us (15%)
  matrix products  204 us (14%)
  local copies, waits for them, and re-layouts  182 us (12%)
  between operations  59.3 us (4%)
  Pallas kernels  27.9 us (2%)
    ppermute x40, waiting for transfers between devices, line_hop(): return lax.ppermute(value, ('dp', 'mp'), moves)  157 us
    ppermute x40, starting transfers between devices, line_hop(): return lax.ppermute(value, ('dp', 'mp'), moves)  152 us
    ppermute x7, waiting for transfers between devices, dp_pair(): return lax.ppermute(value, 'dp', [(d, d ^ 1) for d in range(size)])  142 us
    dynamic_slice x24, other arithmetic, window(): return (start, lax.dynamic_slice_in_dim(store, start, chunk, 0))  121 us
    dot_general x8, matrix products, dot_first(): lax.dot_general(left, right, (((0,), (0,)), ((), ())), preferred_element_...  63.8 us
    dot_general x7, matrix products, dot_plain(): return jnp.dot(left, right, preferred_element_type=F32)  62 us
    dot_general x5, matrix products, dot_t(): lax.dot_general(left, right, (((1,), (1,)), ((), ())), preferred_element_...  55.8 us
    dynamic_update_slice x20, other arithmetic, put(): return lax.dynamic_update_slice_in_dim(store, new, start, 0)  55.7 us
  transfers between devices with their start and end apart: 78, of which 35 were waited for; matrix products, arithmetic and copies ran while one was open for 38% of the time, Pallas kernels for 0%

profile of v3, /device:TPU:0, one launch (start us, length us, event | category | flops | bytes accessed | tf_op | source)
XLA Modules:
  0.0 1448.8 jit_solution(16490490206782020280)
XLA Ops:
  23.4 10.0 gather_fusion.8
  130.5 10.0 convert_reduce_fusion
  173.5 12.4 collective-permute-start.43
  263.6 25.4 %collective-permute-done.38 = bf16[13,56,1120]{2,1,0:T(8,128)(2,1)S(1)} collective-permute-done((bf16[13,56,1120]{2,1,0:T(8,128)(2,1)S(1)}, bf16[13,56,1120]{2,1,0:T(8,128)(2,1)S(1)}, u32[]{:S(2)}, u32[]{:S(2)}) %collective-permute-start.38) | collective-permute-done | bytes 1630752 | tf_op jit(solution)/shard_map/ppermute | solution.py:33
  383.8 36.3 %collective-permute-done.48 = bf16[26,56,1120]{2,1,0:T(8,128)(2,1)} collective-permute-done((bf16[26,56,1120]{2,1,0:T(8,128)(2,1)}, bf16[26,56,1120]{2,1,0:T(8,128)(2,1)}, u32[]{:S(2)}, u32[]{:S(2)}) %collective-permute-start.48) | collective-permute-done | bytes 3261472 | tf_op jit(solution)/shard_map/ppermute | solution.py:33
  471.7 23.5 %collective-permute-done.58 = bf16[21,56,1120]{2,1,0:T(8,128)(2,1)} collective-permute-done((bf16[21,56,1120]{2,1,0:T(8,128)(2,1)}, bf16[21,56,1120]{2,1,0:T(8,128)(2,1)}, u32[]{:S(2)}, u32[]{:S(2)}) %collective-permute-start.58) | collective-permute-done | bytes 2634272 | tf_op jit(solution)/shard_map/ppermute | solution.py:44
  555.2 22.9 %collective-permute-done.60 = bf16[21,56,1120]{2,1,0:T(8,128)(2,1)S(1)} collective-permute-done((bf16[21,56,1120]{2,1,0:T(8,128)(2,1)S(1)}, bf16[21,56,1120]{2,1,0:T(8,128)(2,1)S(1)}, u32[]{:S(2)}, u32[]{:S(2)}) %collective-permute-start.60) | collective-permute-done | bytes 2634272 | tf_op jit(solution)/shard_map/ppermute | solution.py:44
  602.8 16.5 %collective-permute-done.61 = bf16[21,56,1120]{2,1,0:T(8,128)(2,1)} collective-permute-done((bf16[21,56,1120]{2,1,0:T(8,128)(2,1)}, bf16[21,56,1120]{2,1,0:T(8,128)(2,1)}, u32[]{:S(2)}, u32[]{:S(2)}) %collective-permute-start.61) | collective-permute-done | bytes 2634272 | tf_op jit(solution)/shard_map/ppermute | solution.py:44
  624.2 41.4 %select_reduce_fusion.11 = (f32[2048]{0:T(1024)S(1)}, f32[2048,6272]{1,0:T(8,128)}) fusion(pred[6272]{0:T(1024)(128)(4,1)S(1)} %iota_compare_fusion.36, bf16[6272,1120]{1,0:T(8,128)(2,1)} %bitcast.66, bf16[512,1120]{0,1:T(8,128)(2,1)S(1)} %copy-done.42, bf16[512,1120]{0,1:T(8,128)(2,1)S(1)} %get-tuple-element.3421, ...), kind=kOutput, calls=%fused_computation.197 | convolution fusion | flops 28812376064 | bytes 70031488 | tf_op jit(solution)/shard_map/dot_general | solution.py:370
  665.6 18.1 %select_reduce_fusion.10 = (f32[2048]{0:T(1024)S(1)}, f32[2048]{0:T(1024)S(1)}) fusion(f32[2048,6272]{1,0:T(8,128)} %get-tuple-element.3506, f32[2048]{0:T(1024)S(1)} %get-tuple-element.3505, pred[6272]{0:T(1024)(128)(4,1)S(1)} %iota_compare_fusion.36, s32[2048]{0:T(1024)S(1)} %fusion.132), kind=kLoop, calls=%fused_computation.196 | loop fusion | flops 77066240 | bytes 51419264 | tf_op jit(solution)/shard_map/reduce_sum | solution.py:638
  694.7 26.8 %multiply_convert_fusion.1 = bf16[2048,6272]{1,0:T(8,128)(2,1)} fusion(f32[2048,6272]{1,0:T(8,128)} %get-tuple-element.3506, f32[2048]{0:T(1024)} %log_add_fusion, s32[2048]{0:T(1024)S(1)} %get-tuple-element.5691, f32[2048]{0:T(1024)S(1)} %bitcast.402, pred[6272]{0:T(1024)(128)(4,1)S(1)} %copy-done.112), kind=kLoop, calls=%fused_computation.193 | loop fusion | flops 89915392 | bytes 77101184 | tf_op jit(solution)/shard_map/convert_element_type | solution.py:644
  721.6 41.1 %fusion.198 = f32[2,1024,1120]{1,2,0:T(8,128)S(1)} fusion(bf16[2,1024,6272]{2,1,0:T(8,128)(2,1)} %bitcast.361, bf16[6272,1120,1]{1,0,2:T(8,128)(2,1)} %bitcast.82), kind=kOutput, calls=%fused_computation.840 | convolution fusion | flops 28772925440 | bytes 48914432 | tf_op jit(solution)/shard_map/dot_general | solution.py:378
  768.8 36.9 %convolution_convert_fusion.1 = bf16[6272,1120]{1,0:T(8,128)(2,1)S(1)} fusion(bf16[2048,6272]{1,0:T(8,128)(2,1)} %multiply_convert_fusion.1, bf16[512,1120]{0,1:T(8,128)(2,1)S(1)} %copy-done.43, bf16[512,1120]{0,1:T(8,128)(2,1)S(1)} %copy-done.40, bf16[1024,1120]{0,1:T(8,128)(2,1)S(1)} %copy-done.23), kind=kOutput, calls=%fused_computation.200 | convolution fusion | flops 28793712640 | bytes 44326912 | tf_op jit(solution)/shard_map/dot_general | solution.py:374
  828.2 18.8 %collective-permute-done.66 = bf16[512,1120]{0,1:T(8,128)(2,1)} collective-permute-done((bf16[512,1120]{0,1:T(8,128)(2,1)}, bf16[512,1120]{0,1:T(8,128)(2,1)}, u32[]{:S(2)}, u32[]{:S(2)}) %collective-permute-start.66) | collective-permute-done | bytes 1146912 | tf_op jit(solution)/shard_map/ppermute | solution.py:33
  882.4 13.6 collective-permute-done.76
  936.5 11.2 gather_fusion.9
  980.7 44.7 %collective-permute-done.83 = bf16[26,56,1120]{2,1,0:T(8,128)(2,1)} collective-permute-done((bf16[26,56,1120]{2,1,0:T(8,128)(2,1)}, bf16[26,56,1120]{2,1,0:T(8,128)(2,1)}, u32[]{:S(2)}, u32[]{:S(2)}) %collective-permute-start.83) | collective-permute-done | bytes 3261472 | tf_op jit(solution)/shard_map/ppermute | solution.py:33
  1049.5 9.8 collective-permute-start.85
  1069.8 15.5 %collective-permute-done.85 = bf16[9,56,1120]{2,1,0:T(8,128)(2,1)S(1)} collective-permute-done((bf16[9,56,1120]{2,1,0:T(8,128)(2,1)S(1)}, bf16[9,56,1120]{2,1,0:T(8,128)(2,1)S(1)}, u32[]{:S(2)}, u32[]{:S(2)}) %collective-permute-start.85) | collective-permute-done | bytes 1128992 | tf_op jit(solution)/shard_map/ppermute | solution.py:44
  1118.2 9.9 collective-permute-done.86
  1214.4 14.0 collective-permute-done.90
  1247.3 10.7 collective-permute-done.91
  1360.6 27.9 %shard_map.169 = (f32[42,56,1120]{2,1,0:T(8,128)}, f32[8,1120]{1,0:T(8,128)}) custom-call(s32[42]{0:T(128)} %get-tuple-element.3500.kind_ref, s32[42]{0:T(128)} %select_reduce_fusion.23.e_at, s32[42]{0:T(128)} %get-tuple-element.3511.f_at, s32[42]{0:T(128)} %get-tuple-element.3510.a_at, f32[42,56,1120]{2,1,0:T(8,128)} %bitcast.334, ...), custom_call_target="tpu_custom_call" | custom-call | tf_op jit(solution)/shard_map/pallas_call | solution.py:422
  1420.0 27.2 %multiply_subtract_fusion = (f32[42,56,1120]{2,1,0:T(8,128)}, f32[42,56,1120]{2,1,0:T(8,128)}, f32[42,56,1120]{2,1,0:T(8,128)}) fusion(f32[42,56,1120]{2,1,0:T(8,128)} %param.52, f32[42,56,1120]{2,1,0:T(8,128)} %get-tuple-element.2720, f32[]{:T(128)S(6)} %min.858, f32[42,56,1120]{2,1,0:T(8,128)} %param.53, f32[42,56,1120]{2,1,0:T(8,128)} %param.54), kind=kLoop, calls=%fused_computation.203 | loop fusion | flops 42147840 | bytes 73758720 | tf_op jit(solution)/shard_map/sub | solution.py:457
  (993 shorter events, 864.8 us)
Async XLA Ops:
  37.0 196.6 %collective-permute-start.54 = (bf16[21,56,1120]{2,1,0:T(8,128)(2,1)}, bf16[21,56,1120]{2,1,0:T(8,128)(2,1)}, u32[]{:S(2)}, u32[]{:S(2)}) collective-permute-start(bf16[21,56,1120]{2,1,0:T(8,128)(2,1)} %constant_dynamic-slice_fusion.36), channel_id=1, source_target_pairs={{0,8},{2,10},{4,12},{6,14},{8,16},{9,1},{10,18},{11,3},{12,20},{13... | collective-permute-start | bytes 7902728 | tf_op jit(solution)/shard_map/ppermute | solution.py:44
  43.5 68.3 %collective-permute-start.26 = (s32[1,2,1028]{2,1,0:T(2,128)S(1)}, s32[1,2,1028]{2,1,0:T(2,128)S(1)}, u32[]{:S(2)}, u32[]{:S(2)}) collective-permute-start(s32[1,2,1028]{2,1,0:T(2,128)S(1)} %bitcast.405), channel_id=1, source_target_pairs={{0,4},{4,0},{8,12},{12,8},{16,20},{20,16},{24,28},{28,24},{1,5},{5... | collective-permute-start | bytes 24680 | tf_op jit(solution)/shard_map/ppermute | solution.py:49
  62.9 78.9 %collective-permute-start.32 = (bf16[5,56,1120]{2,1,0:T(8,128)(2,1)}, bf16[5,56,1120]{2,1,0:T(8,128)(2,1)}, u32[]{:S(2)}, u32[]{:S(2)}) collective-permute-start(bf16[5,56,1120]{2,1,0:T(8,128)(2,1)} %constant_dynamic-slice_fusion.57), channel_id=1, source_target_pairs={{0,8},{2,10},{4,12},{6,14},{8,16},{9,1},{10,18},{11,3},{12,20},{13... | collective-permute-start | bytes 1881608 | tf_op jit(solution)/shard_map/ppermute | solution.py:44
  86.2 83.6 %collective-permute-start.42 = (bf16[9,56,1120]{2,1,0:T(8,128)(2,1)}, bf16[9,56,1120]{2,1,0:T(8,128)(2,1)}, u32[]{:S(2)}, u32[]{:S(2)}) collective-permute-start(bf16[9,56,1120]{2,1,0:T(8,128)(2,1)} %constant_dynamic-slice_fusion.46), channel_id=1, source_target_pairs={{0,8},{2,10},{4,12},{6,14},{8,16},{9,1},{10,18},{11,3},{12,20},{13... | collective-permute-start | bytes 3386888 | tf_op jit(solution)/shard_map/ppermute | solution.py:44
  240.3 87.8 %collective-permute-start.55 = (bf16[21,56,1120]{2,1,0:T(8,128)(2,1)}, bf16[21,56,1120]{2,1,0:T(8,128)(2,1)}, u32[]{:S(2)}, u32[]{:S(2)}) collective-permute-start(bf16[21,56,1120]{2,1,0:T(8,128)(2,1)} %get-tuple-element.3381), channel_id=1, source_target_pairs={{1,9},{3,11},{5,13},{7,15},{8,0},{9,17},{10,2},{11,19},{12,4},{13,... | collective-permute-start | bytes 7902728 | tf_op jit(solution)/shard_map/ppermute | solution.py:44
  256.1 64.1 %collective-permute-start.46 = (bf16[9,56,1120]{2,1,0:T(8,128)(2,1)}, bf16[9,56,1120]{2,1,0:T(8,128)(2,1)}, u32[]{:S(2)}, u32[]{:S(2)}) collective-permute-start(bf16[9,56,1120]{2,1,0:T(8,128)(2,1)} %get-tuple-element.3393), channel_id=1, source_target_pairs={{0,8},{2,10},{4,12},{6,14},{8,16},{9,1},{10,18},{11,3},{12,20},{13... | collective-permute-start | bytes 3386888 | tf_op jit(solution)/shard_map/ppermute | solution.py:44
  352.0 68.2 %collective-permute-start.48 = (bf16[26,56,1120]{2,1,0:T(8,128)(2,1)}, bf16[26,56,1120]{2,1,0:T(8,128)(2,1)}, u32[]{:S(2)}, u32[]{:S(2)}) collective-permute-start(bf16[26,56,1120]{2,1,0:T(8,128)(2,1)} %constant_dynamic-slice_fusion.39), channel_id=1, source_target_pairs={{0,4},{4,0},{8,12},{12,8},{16,20},{20,16},{24,28},{28,24},{1,5},{5... | collective-permute-start | bytes 9784328 | tf_op jit(solution)/shard_map/ppermute | solution.py:33
  376.3 77.5 %collective-permute-start.57 = (bf16[21,56,1120]{2,1,0:T(8,128)(2,1)}, bf16[21,56,1120]{2,1,0:T(8,128)(2,1)}, u32[]{:S(2)}, u32[]{:S(2)}) collective-permute-start(bf16[21,56,1120]{2,1,0:T(8,128)(2,1)} %get-tuple-element.3377), channel_id=1, source_target_pairs={{1,9},{3,11},{5,13},{7,15},{8,0},{9,17},{10,2},{11,19},{12,4},{13,... | collective-permute-start | bytes 7902728 | tf_op jit(solution)/shard_map/ppermute | solution.py:44
  381.8 54.2 %collective-permute-start.41 = (f32[512,1120]{0,1:T(8,128)}, f32[512,1120]{0,1:T(8,128)}, u32[]{:S(2)}, u32[]{:S(2)}) collective-permute-start(f32[512,1120]{0,1:T(8,128)} %convert_add_fusion.4), channel_id=1, source_target_pairs={{0,1},{1,0},{2,3},{3,2},{4,5},{5,4},{6,7},{7,6},{8,9},{9,8},{10,11... | collective-permute-start | bytes 6881288 | tf_op jit(solution)/shard_map/ppermute | solution.py:54
  768.8 45.2 %collective-permute-start.65 = (f32[2,512,1120]{1,2,0:T(8,128)}, f32[2,512,1120]{1,2,0:T(8,128)}, u32[]{:S(2)}, u32[]{:S(2)}) collective-permute-start(f32[2,512,1120]{1,2,0:T(8,128)} %constant_dynamic-slice_fusion.27), channel_id=1, source_target_pairs={{0,1},{1,0},{2,3},{3,2},{4,5},{5,4},{6,7},{7,6},{8,9},{9,8},{10,11... | collective-permute-start | bytes 13762568 | tf_op jit(solution)/shard_map/ppermute | solution.py:54
  902.8 65.3 %collective-permute-start.77 = (bf16[21,56,1120]{2,1,0:T(8,128)(2,1)}, bf16[21,56,1120]{2,1,0:T(8,128)(2,1)}, u32[]{:S(2)}, u32[]{:S(2)}) collective-permute-start(bf16[21,56,1120]{2,1,0:T(8,128)(2,1)} %get-tuple-element.3365), channel_id=1, source_target_pairs={{1,9},{3,11},{5,13},{7,15},{8,0},{9,17},{10,2},{11,19},{12,4},{13,... | collective-permute-start | bytes 7902728 | tf_op jit(solution)/shard_map/ppermute | solution.py:44
  953.0 72.4 %collective-permute-start.83 = (bf16[26,56,1120]{2,1,0:T(8,128)(2,1)}, bf16[26,56,1120]{2,1,0:T(8,128)(2,1)}, u32[]{:S(2)}, u32[]{:S(2)}) collective-permute-start(bf16[26,56,1120]{2,1,0:T(8,128)(2,1)} %dynamic-slice_convert_fusion.8), channel_id=1, source_target_pairs={{0,4},{4,0},{8,12},{12,8},{16,20},{20,16},{24,28},{28,24},{1,5},{5... | collective-permute-start | bytes 9784328 | tf_op jit(solution)/shard_map/ppermute | solution.py:33
  975.1 62.8 %collective-permute-start.78 = (bf16[21,56,1120]{2,1,0:T(8,128)(2,1)}, bf16[21,56,1120]{2,1,0:T(8,128)(2,1)}, u32[]{:S(2)}, u32[]{:S(2)}) collective-permute-start(bf16[21,56,1120]{2,1,0:T(8,128)(2,1)} %get-tuple-element.3363), channel_id=1, source_target_pairs={{0,8},{2,10},{4,12},{6,14},{8,16},{9,1},{10,18},{11,3},{12,20},{13... | collective-permute-start | bytes 7902728 | tf_op jit(solution)/shard_map/ppermute | solution.py:44
  980.2 79.1 %collective-permute-start.70 = (bf16[512,1120]{0,1:T(8,128)(2,1)}, bf16[512,1120]{0,1:T(8,128)(2,1)}, u32[]{:S(2)}, u32[]{:S(2)}) collective-permute-start(bf16[512,1120]{0,1:T(8,128)(2,1)} %fusion.101), channel_id=1, source_target_pairs={{0,2},{1,3},{2,0},{3,1},{4,6},{5,7},{6,4},{7,5},{8,10},{9,11},{10,... | collective-permute-start | bytes 3440648 | tf_op jit(solution)/shard_map/ppermute | solution.py:54
  1044.9 58.5 %collective-permute-start.79 = (bf16[21,56,1120]{2,1,0:T(8,128)(2,1)}, bf16[21,56,1120]{2,1,0:T(8,128)(2,1)}, u32[]{:S(2)}, u32[]{:S(2)}) collective-permute-start(bf16[21,56,1120]{2,1,0:T(8,128)(2,1)} %get-tuple-element.3361), channel_id=1, source_target_pairs={{1,9},{3,11},{5,13},{7,15},{8,0},{9,17},{10,2},{11,19},{12,4},{13,... | collective-permute-start | bytes 7902728 | tf_op jit(solution)/shard_map/ppermute | solution.py:44
  1062.0 88.2 %collective-permute-start.71 = (f32[512,1120]{0,1:T(8,128)S(1)}, f32[512,1120]{0,1:T(8,128)S(1)}, u32[]{:S(2)}, u32[]{:S(2)}) collective-permute-start(f32[512,1120]{0,1:T(8,128)S(1)} %convert_add_fusion.1), channel_id=1, source_target_pairs={{0,1},{1,0},{2,3},{3,2},{4,5},{5,4},{6,7},{7,6},{8,9},{9,8},{10,11... | collective-permute-start | bytes 6881288 | tf_op jit(solution)/shard_map/ppermute | solution.py:54
  1068.5 59.6 %collective-permute-start.86 = (bf16[9,56,1120]{2,1,0:T(8,128)(2,1)S(1)}, bf16[9,56,1120]{2,1,0:T(8,128)(2,1)S(1)}, u32[]{:S(2)}, u32[]{:S(2)}) collective-permute-start(bf16[9,56,1120]{2,1,0:T(8,128)(2,1)S(1)} %dynamic-slice_convert_fusion.13), channel_id=1, source_target_pairs={{1,9},{3,11},{5,13},{7,15},{8,0},{9,17},{10,2},{11,19},{12,4},{13,... | collective-permute-start | bytes 3386888 | tf_op jit(solution)/shard_map/ppermute | solution.py:44
  1090.4 45.2 %collective-permute-start.87 = (bf16[9,56,1120]{2,1,0:T(8,128)(2,1)S(1)}, bf16[9,56,1120]{2,1,0:T(8,128)(2,1)S(1)}, u32[]{:S(2)}, u32[]{:S(2)}) collective-permute-start(bf16[9,56,1120]{2,1,0:T(8,128)(2,1)S(1)} %dynamic-slice_convert_fusion.12), channel_id=1, source_target_pairs={{0,8},{2,10},{4,12},{6,14},{8,16},{9,1},{10,18},{11,3},{12,20},{13... | collective-permute-start | bytes 3386888 | tf_op jit(solution)/shard_map/ppermute | solution.py:44
  1110.1 92.1 %collective-permute-start.80 = (bf16[21,56,1120]{2,1,0:T(8,128)(2,1)}, bf16[21,56,1120]{2,1,0:T(8,128)(2,1)}, u32[]{:S(2)}, u32[]{:S(2)}) collective-permute-start(bf16[21,56,1120]{2,1,0:T(8,128)(2,1)} %get-tuple-element.3359), channel_id=1, source_target_pairs={{0,8},{2,10},{4,12},{6,14},{8,16},{9,1},{10,18},{11,3},{12,20},{13... | collective-permute-start | bytes 7902728 | tf_op jit(solution)/shard_map/ppermute | solution.py:44
  1134.3 76.5 %collective-permute-start.88 = (bf16[9,56,1120]{2,1,0:T(8,128)(2,1)}, bf16[9,56,1120]{2,1,0:T(8,128)(2,1)}, u32[]{:S(2)}, u32[]{:S(2)}) collective-permute-start(bf16[9,56,1120]{2,1,0:T(8,128)(2,1)} %dynamic-slice_convert_fusion.11), channel_id=1, source_target_pairs={{1,9},{3,11},{5,13},{7,15},{8,0},{9,17},{10,2},{11,19},{12,4},{13,... | collective-permute-start | bytes 3386888 | tf_op jit(solution)/shard_map/ppermute | solution.py:44
  1142.0 93.1 %collective-permute-start.89 = (bf16[9,56,1120]{2,1,0:T(8,128)(2,1)}, bf16[9,56,1120]{2,1,0:T(8,128)(2,1)}, u32[]{:S(2)}, u32[]{:S(2)}) collective-permute-start(bf16[9,56,1120]{2,1,0:T(8,128)(2,1)} %dynamic-slice_convert_fusion.10), channel_id=1, source_target_pairs={{0,8},{2,10},{4,12},{6,14},{8,16},{9,1},{10,18},{11,3},{12,20},{13... | collective-permute-start | bytes 3386888 | tf_op jit(solution)/shard_map/ppermute | solution.py:44
  1201.2 42.7 %collective-permute-start.72 = (f32[512,1120]{0,1:T(8,128)}, f32[512,1120]{0,1:T(8,128)}, u32[]{:S(2)}, u32[]{:S(2)}) collective-permute-start(f32[512,1120]{0,1:T(8,128)} %constant_dynamic-slice_fusion.25), channel_id=1, source_target_pairs={{0,1},{1,0},{2,3},{3,2},{4,5},{5,4},{6,7},{7,6},{8,9},{9,8},{10,11... | collective-permute-start | bytes 6881288 | tf_op jit(solution)/shard_map/ppermute | solution.py:54
  1209.3 79.6 %collective-permute-start.81 = (bf16[21,56,1120]{2,1,0:T(8,128)(2,1)}, bf16[21,56,1120]{2,1,0:T(8,128)(2,1)}, u32[]{:S(2)}, u32[]{:S(2)}) collective-permute-start(bf16[21,56,1120]{2,1,0:T(8,128)(2,1)} %get-tuple-element.3357), channel_id=1, source_target_pairs={{1,9},{3,11},{5,13},{7,15},{8,0},{9,17},{10,2},{11,19},{12,4},{13,... | collective-permute-start | bytes 7902728 | tf_op jit(solution)/shard_map/ppermute | solution.py:44
  1295.8 40.5 %collective-permute-start.82 = (bf16[21,56,1120]{2,1,0:T(8,128)(2,1)}, bf16[21,56,1120]{2,1,0:T(8,128)(2,1)}, u32[]{:S(2)}, u32[]{:S(2)}) collective-permute-start(bf16[21,56,1120]{2,1,0:T(8,128)(2,1)} %get-tuple-element.3355), channel_id=1, source_target_pairs={{0,8},{2,10},{4,12},{6,14},{8,16},{9,1},{10,18},{11,3},{12,20},{13... | collective-permute-start | bytes 7902728 | tf_op jit(solution)/shard_map/ppermute | solution.py:44
  (281 other events, 4775.7 us)
